TPU v7x, 32 devices: a whole 2x2x4 slice. The times are simulated.
32 devices in a mesh: tp: 4 (over z), ep: 8 (over y, x, core).
Axes of the slice: x: 2, y: 2, z: 4, core: 2. Of those that a mesh axis runs over, the one named last changes fastest.
Arguments:
- hidden_in: bfloat16 [4096, 3584], P(('ep', 'tp')), may hold values from -6 to 6
- cotangent: bfloat16 [4096, 3584], P(('ep', 'tp')), may hold values from -8 to 8
- routes: int32 [4096, 2], P(('ep', 'tp')), may hold values from 0 to 63, all different within a row; in each aligned block of 128 rows (0 to 127, 128 to 255, ...) at most 4 rows name the same one
- gate_values: float32 [4096, 2], P(('ep', 'tp')), may hold values from 0.25 to 1
- dense_gate: bfloat16 [2432, 3584], P('tp'), may hold values from -0.09375 to 0.09375
- dense_up: bfloat16 [2432, 3584], P('tp'), may hold values from -0.09375 to 0.09375
- dense_down: bfloat16 [2432, 3584], P('tp', 'ep'), may hold values from -0.125 to 0.125
- expert_gate: bfloat16 [4, 4864, 3584], P('tp', 'ep'), may hold values from -0.09375 to 0.09375
- expert_up: bfloat16 [4, 4864, 3584], P('tp', 'ep'), may hold values from -0.09375 to 0.09375
- expert_down: bfloat16 [4, 4864, 3584], P('tp', 'ep'), may hold values from -0.078125 to 0.078125
Outputs:
- grad_input: bfloat16 [4096, 3584], P(('ep', 'tp'))
- grad_dense_gate: bfloat16 [2432, 3584], P('tp', 'ep')
- grad_dense_up: bfloat16 [2432, 3584], P('tp', 'ep')
- grad_dense_down: bfloat16 [2432, 3584], P('tp', 'ep')
- grad_expert_gate: bfloat16 [4, 4864, 3584], P('tp', 'ep')
- grad_expert_up: bfloat16 [4, 4864, 3584], P('tp', 'ep')
- grad_expert_down: bfloat16 [4, 4864, 3584], P('tp', 'ep')
Inputs may be any that keep to these rules, and one draw needn't show every extreme that they name: `routes`: the two experts of a token differ. Among the tokens of one aligned block of 128 rows no expert is named more than 4 times, a bound that some block reaches; every expert is named somewhere.
All inputs are finite; a program needn't handle non-finite values.
Results may differ from a plain program's by a relative error of at most 0.012.
Values may be sent and summed in bfloat16 or wider, within the bound.
No kernel may reach another device: no remote copies, remote signals or barrier semaphores. Data moves between devices by JAX's collectives and lax.ppermute only.
A program may use at most 192 MiB of HBM per device.

v0:
```python
import jax
import jax.numpy as jnp
from jax import lax
from jax.experimental import pallas as pl
from jax.experimental.pallas import tpu as pltpu
from jax.sharding import PartitionSpec as P

CAP = 4
CONTRACT = (((1,), (1,)), ((), ()))
LEADING = (((0,), (0,)), ((), ()))
F32 = jnp.float32
BF16 = jnp.bfloat16


def swiglu_backward(gate_pre, up_pre, grad_act):
    sigmoid_gate = jax.nn.sigmoid(gate_pre)
    silu_gate = gate_pre * sigmoid_gate
    act = (silu_gate * up_pre).astype(BF16)
    silu_slope = sigmoid_gate * (1.0 + gate_pre * (1.0 - sigmoid_gate))
    grad_gate = (grad_act * up_pre * silu_slope).astype(BF16)
    grad_up = (grad_act * silu_gate).astype(BF16)
    return act, grad_gate, grad_up


def slot_tables(routes, gate_values, me, experts):
    tok_count = routes.shape[0]
    named = lax.rem(me + jnp.arange(experts, dtype=jnp.int32), experts)
    onehot = (routes.reshape(-1)[:, None] == named[None, :]).astype(jnp.int32)
    before = jnp.cumsum(onehot, axis=0) - onehot
    slot = onehot[:, :, None] * (before[:, :, None] == jnp.arange(CAP, dtype=jnp.int32)).astype(
        jnp.int32
    )
    slot = slot.reshape(tok_count, 2, experts * CAP).astype(F32)
    dispatch = jnp.sum(slot, axis=1).T.astype(BF16)
    weight = jnp.sum(slot * gate_values[:, :, None], axis=(0, 1))
    return dispatch, weight


def shift(x, axis, size, by):
    return lax.ppermute(x, axis, [(i, (i + by) % size) for i in range(size)])


def slots_to_send(hidden_in, cotangent, dispatch, weight, experts):
    width = hidden_in.shape[1]
    rows = jnp.dot(dispatch, hidden_in, preferred_element_type=F32).astype(BF16)
    cots = jnp.dot(dispatch, cotangent, preferred_element_type=F32)
    cots = (cots * weight[:, None]).astype(BF16)
    return jnp.stack(
        [rows.reshape(experts, CAP, width), cots.reshape(experts, CAP, width)], axis=1
    )


def exchange_slots(sent, me, experts):
    width = sent.shape[3]
    sent = jnp.roll(sent, me, axis=0)
    got = lax.all_to_all(sent, "tp", split_axis=0, concat_axis=0, tiled=True)
    return got.transpose(1, 0, 2, 3).reshape(2, experts * CAP, width)


def expert_layer(slot_rows, slot_cot, gate_weight, up_weight, down_weight):
    e_gate = lax.dot_general(slot_rows, gate_weight, CONTRACT, preferred_element_type=F32)
    e_up = lax.dot_general(slot_rows, up_weight, CONTRACT, preferred_element_type=F32)
    e_grad_act = lax.dot_general(slot_cot, down_weight, CONTRACT, preferred_element_type=F32)
    e_act, e_grad_gate, e_grad_up = swiglu_backward(e_gate, e_up, e_grad_act)
    g_down = lax.dot_general(e_act, slot_cot, LEADING, preferred_element_type=F32).astype(BF16)
    g_gate = lax.dot_general(e_grad_gate, slot_rows, LEADING, preferred_element_type=F32).astype(
        BF16
    )
    g_up = lax.dot_general(e_grad_up, slot_rows, LEADING, preferred_element_type=F32).astype(BF16)
    terms = jnp.dot(e_grad_gate, gate_weight, preferred_element_type=F32) + jnp.dot(
        e_grad_up, up_weight, preferred_element_type=F32
    )
    return g_gate, g_up, g_down, terms.astype(BF16)


def slots_back(own, dispatch, me, experts):
    width = own.shape[1]
    own = own.reshape(experts, CAP, width)
    back = [
        lax.dynamic_index_in_dim(own, lax.rem(me - k + experts, experts), keepdims=False)
        for k in range(experts)
    ]
    back = jnp.stack(back[:1] + [shift(back[k], "tp", experts, -k) for k in range(1, experts)])
    return lax.dot_general(
        dispatch, back.reshape(experts * CAP, width), LEADING, preferred_element_type=F32
    )


def plain_block(rows, cot, gate, up, down):
    gate_pre = lax.dot_general(rows, gate, CONTRACT, preferred_element_type=F32)
    up_pre = lax.dot_general(rows, up, CONTRACT, preferred_element_type=F32)
    grad_act = lax.dot_general(cot, down, CONTRACT, preferred_element_type=F32)
    act, grad_gate, grad_up = swiglu_backward(gate_pre, up_pre, grad_act)
    partial = jnp.dot(grad_gate, gate, preferred_element_type=F32) + jnp.dot(
        grad_up, up, preferred_element_type=F32
    )
    return act, grad_gate, grad_up, partial.astype(BF16)


VMEM_LIMIT = 24 * 1024 * 1024
VMEM_ALL = 60 * 1024 * 1024


def unit_tiles(units):
    return [(start, min(256, units - start)) for start in range(0, units, 256)]


def layer_kernel(rows, cots, gate, up, down, down_turned, turned, partial, col):
    units, width = gate.shape
    for start, size in unit_tiles(units):
        gate_pre, up_pre = [
            lax.dot_general(w[start : start + size], rows, CONTRACT, preferred_element_type=F32)
            for w in (gate, up)
        ]
        if down_turned:
            grad_act = jnp.dot(
                cots, down[:, start : start + size], preferred_element_type=F32
            ).T
        else:
            grad_act = lax.dot_general(
                down[start : start + size], cots, CONTRACT, preferred_element_type=F32
            )
        for i, value in enumerate(swiglu_backward(gate_pre, up_pre, grad_act)):
            turned[i, start : start + size] = value
    grads = [turned[1].T, turned[2].T]
    for j in range(0, width, col):
        partial[:, j : j + col] = (
            jnp.dot(grads[0], gate[:, j : j + col], preferred_element_type=F32)
            + jnp.dot(grads[1], up[:, j : j + col], preferred_element_type=F32)
        ).astype(BF16)


def dense_block(core, blocks, gate, up, down):
    tok, width = blocks[0].shape[1] * len(blocks), blocks[0].shape[2]
    units = gate.shape[0]
    half = units // 2

    def kernel(core_ref, *refs):
        ins, refs = refs[: len(blocks)], refs[len(blocks) :]
        gate, up, down, own, other, partial, turned = refs
        rows, cots = [
            ins[0][k]
            if len(ins) == 1
            else jnp.concatenate([ref[k] for ref in ins], axis=0)
            for k in range(2)
        ]
        layer_kernel(rows, cots, gate, up, down, True, turned, partial, 512)
        mine = core_ref[0]
        own[...] = turned[:, pl.ds(pl.multiple_of(mine * half, 16), half), :]
        other[...] = turned[:, pl.ds(pl.multiple_of((1 - mine) * half, 16), half), :]

    vmem = pl.BlockSpec(memory_space=pltpu.VMEM)
    return pl.pallas_call(
        kernel,
        in_specs=[pl.BlockSpec(memory_space=pltpu.SMEM)] + [vmem] * (len(blocks) + 3),
        out_specs=[vmem, vmem, vmem],
        out_shape=[
            jax.ShapeDtypeStruct((3, half, tok), BF16),
            jax.ShapeDtypeStruct((3, half, tok), BF16),
            jax.ShapeDtypeStruct((tok, width), BF16),
        ],
        scratch_shapes=[pltpu.VMEM((3, units, tok), BF16)],
        compiler_params=pltpu.CompilerParams(vmem_limit_bytes=VMEM_LIMIT),
        cost_estimate=pl.CostEstimate(
            flops=10 * units * width * tok,
            bytes_accessed=6 * units * width + 6 * tok * (width + units),
            transcendentals=units * tok,
        ),
        name="dense_block",
    )(core.reshape(1), *blocks, gate, up, down)


def expert_block(rows, cots, gate, up, down):
    tok, width = rows.shape
    units = gate.shape[0]
    col = width // 4

    def kernel(
        rows, cots, gate, up, down, g_gate, g_up, g_down, partial, turned, made, out_sems
    ):
        layer_kernel(rows[...], cots[...], gate, up, down, False, turned, partial, 512)
        outs = (g_down, g_gate, g_up)
        pending = [None, None]
        step = 0
        for i in range(3):
            right = cots if i == 0 else rows
            for j in range(0, width, col):
                slot = step % 2
                if pending[slot] is not None:
                    pending[slot].wait()
                made[slot] = jnp.dot(
                    turned[i], right[:, j : j + col], preferred_element_type=F32
                ).astype(BF16)
                copy = pltpu.make_async_copy(
                    made.at[slot], outs[i].at[:, pl.ds(j, col)], out_sems.at[slot]
                )
                copy.start()
                pending[slot] = copy
                step += 1
        for copy in pending:
            copy.wait()

    vmem = pl.BlockSpec(memory_space=pltpu.VMEM)
    hbm = pl.BlockSpec(memory_space=pl.ANY)
    grad = jax.ShapeDtypeStruct((units, width), BF16)
    return pl.pallas_call(
        kernel,
        in_specs=[vmem] * 5,
        out_specs=[hbm, hbm, hbm, vmem],
        out_shape=[grad, grad, grad, jax.ShapeDtypeStruct((tok, width), BF16)],
        scratch_shapes=[
            pltpu.VMEM((3, units, tok), BF16),
            pltpu.VMEM((2, units, col), BF16),
            pltpu.SemaphoreType.DMA((2,)),
        ],
        compiler_params=pltpu.CompilerParams(vmem_limit_bytes=VMEM_LIMIT),
        cost_estimate=pl.CostEstimate(
            flops=16 * units * width * tok,
            bytes_accessed=12 * units * width + 6 * tok * width,
            transcendentals=units * tok,
        ),
        name="expert_block",
    )(rows, cots, gate, up, down)


def final_sum(core, lows, highs):
    count = len(lows)
    _, cut, width = lows[0].shape
    units = cut + highs[0].shape[1]
    half = width // 2

    def kernel(core_ref, *refs):
        ins, (mine, other) = refs[:-2], refs[-2:]
        own_first = core_ref[0] == 0
        for i in range(3):
            for begin, group in ((0, ins[:count]), (cut, ins[count:])):
                total = group[0][i].astype(F32)
                for ref in group[1:]:
                    total = total + ref[i].astype(F32)
                left, right = total[:, :half].astype(BF16), total[:, half:].astype(BF16)
                size = total.shape[0]
                mine[i, begin : begin + size] = jnp.where(own_first, left, right)
                other[i, begin : begin + size] = jnp.where(own_first, right, left)

    vmem = pl.BlockSpec(memory_space=pltpu.VMEM)
    shape = jax.ShapeDtypeStruct((3, units, half), BF16)
    return pl.pallas_call(
        kernel,
        in_specs=[pl.BlockSpec(memory_space=pltpu.SMEM)] + [vmem] * (2 * count),
        out_specs=[vmem, vmem],
        out_shape=[shape, shape],
        compiler_params=pltpu.CompilerParams(vmem_limit_bytes=VMEM_LIMIT),
        cost_estimate=pl.CostEstimate(
            flops=3 * count * units * width,
            bytes_accessed=6 * (count + 1) * units * width,
            transcendentals=0,
        ),
        name="final_sum",
    )(core.reshape(1), *lows, *highs)


def join_halves(core, mine, other):
    _, units, width = mine.shape

    def kernel(core_ref, mine, other, *outs):
        first = core_ref[0] == 0
        for i in range(3):
            a, b = mine[i], other[i]
            joined = jnp.concatenate([jnp.where(first, a, b), jnp.where(first, b, a)], axis=0)
            outs[i][...] = joined.T

    vmem = pl.BlockSpec(memory_space=pltpu.VMEM)
    grads = pl.pallas_call(
        kernel,
        in_specs=[pl.BlockSpec(memory_space=pltpu.SMEM), vmem, vmem],
        out_specs=[vmem] * 3,
        out_shape=[jax.ShapeDtypeStruct((width, 2 * units), BF16)] * 3,
        compiler_params=pltpu.CompilerParams(vmem_limit_bytes=VMEM_ALL),
        cost_estimate=pl.CostEstimate(
            flops=0, bytes_accessed=24 * units * width, transcendentals=0
        ),
        name="join_halves",
    )(core.reshape(1), mine, other)
    return [grad.T for grad in grads]


def weight_terms(tile, acts, blocks, width, cut):
    units = acts[0].shape[1]
    tokens = sum(b.shape[1] for b in blocks)

    def kernel(tile_ref, *refs):
        a, b = refs[: len(acts)], refs[len(acts) : -2]
        low, high = refs[-2:]
        rows = jnp.concatenate([ref[0] for ref in b], axis=0)
        cots = jnp.concatenate([ref[1] for ref in b], axis=0)
        for i in range(3):
            left = jnp.concatenate([ref[i] for ref in a], axis=1)
            made = jnp.dot(left, cots if i == 0 else rows, preferred_element_type=F32).astype(BF16)
            low[i] = made[:cut]
            high[i] = made[cut:]

    def whole(shape):
        return pl.BlockSpec(shape, lambda i, tile_ref: (0, 0, 0))

    def columns(block):
        return pl.BlockSpec((*block.shape[:2], width), lambda i, tile_ref: (0, 0, tile_ref[0]))

    return pl.pallas_call(
        kernel,
        grid_spec=pltpu.PrefetchScalarGridSpec(
            num_scalar_prefetch=1,
            grid=(1,),
            in_specs=[whole(a.shape) for a in acts] + [columns(b) for b in blocks],
            out_specs=[whole((3, cut, width)), whole((3, units - cut, width))],
        ),
        out_shape=[
            jax.ShapeDtypeStruct((3, cut, width), BF16),
            jax.ShapeDtypeStruct((3, units - cut, width), BF16),
        ],
        compiler_params=pltpu.CompilerParams(vmem_limit_bytes=VMEM_ALL),
        cost_estimate=pl.CostEstimate(
            flops=6 * units * tokens * width,
            bytes_accessed=2 * (tokens * (2 * width + 3 * units) + 3 * units * width),
            transcendentals=0,
        ),
        name="weight_terms",
    )(tile.reshape(1), *acts, *blocks)


def together(*values):
    return lax.optimization_barrier(values)


def line_body(
    hidden_in,
    cotangent,
    routes,
    gate_values,
    dense_gate,
    dense_up,
    dense_down,
    expert_gate,
    expert_up,
    expert_down,
):
    experts = lax.axis_size("tp")
    me = lax.axis_index("tp")
    ep = lax.axis_index("ep")
    core, chip = lax.rem(ep, 2), lax.div(ep, 2)
    half = dense_gate.shape[0] // 2
    columns = dense_down.shape[1]
    own = jnp.stack([hidden_in, cotangent])

    down = lax.all_gather(dense_down.T, "ep", axis=0, tiled=True)

    def pairs(value):
        return lax.ppermute(value, "tp", [(0, 1), (1, 0), (2, 3), (3, 2)])

    def mirror(value):
        return lax.ppermute(value, "tp", [(0, 3), (1, 2), (2, 1), (3, 0)])

    def across(value, apart):
        return lax.ppermute(value, "ep", [(i, i ^ apart) for i in range(8)])

    def add(a, b):
        return (a.astype(F32) + b.astype(F32)).astype(BF16)

    def dense(blocks):
        mine, other, partial = dense_block(core, blocks, dense_gate, dense_up, down)
        tokens = [*blocks, *(across(b, 1) for b in blocks)]
        return ([mine, across(other, 1)], tokens), partial

    mirrored, paired = mirror(own), pairs(own)
    dispatch, weight = slot_tables(routes, gate_values, me, experts)
    sent = slots_to_send(hidden_in, cotangent, dispatch, weight, experts)
    got = exchange_slots(sent, me, experts)
    both0, partial0 = dense([own])

    mirrored, paired, partial0, got = together(mirrored, paired, partial0, got)
    last = pairs(mirrored)
    slots = lax.all_gather(got, "ep", axis=0, tiled=False)
    both12, partial12 = dense([paired, mirrored])
    slots, partial12 = together(slots, partial12)
    slot_rows, slot_cot = slots[:, 0].reshape(-1, hidden_in.shape[1]), slots[:, 1].reshape(
        -1, hidden_in.shape[1]
    )
    g_gate, g_up, g_down, slot_terms = expert_block(
        slot_rows, slot_cot, expert_gate[0], expert_up[0], expert_down[0]
    )

    last, slot_terms, both0, both12 = together(last, slot_terms, both0, both12)
    routed = lax.psum_scatter(slot_terms, "ep", scatter_dimension=0, tiled=True)
    both3, partial3 = dense([last])
    paired_partial, mirrored_partial = jnp.split(partial12, 2, axis=0)
    from_last = pairs(partial3)

    acts, tokens = (a + b + c for a, b, c in zip(both0, both12, both3))
    cut = -(-half // 32) * 16
    made = {3: weight_terms(jnp.bitwise_xor(chip, 3), acts, tokens, 2 * columns, cut)}
    made[3], chip = together(made[3], chip)
    for apart in (1, 2, 0):
        made[apart] = weight_terms(
            jnp.bitwise_xor(chip, apart), acts, tokens, 2 * columns, cut
        )
    low = across(made[3][0], 2)
    high = across(made[3][1], 4)
    low_own = across(made[1][0], 2)
    high_own = across(made[2][1], 4)
    from_last, routed, made[0] = together(from_last, routed, made[0])
    from_mirror = mirror(add(mirrored_partial, from_last))
    from_pair = pairs(paired_partial)
    routed_input = slots_back(routed, dispatch, me, experts)
    low, high, made[0] = together(low, high, made[0])
    low = across(add(made[2][0], low), 4)
    high = across(add(made[1][1], high), 2)
    low, high, from_pair, from_mirror, routed_input = together(
        low, high, from_pair, from_mirror, routed_input
    )
    mine, other = final_sum(
        core, (made[0][0], low_own, low), (made[0][1], high_own, high)
    )
    grads = join_halves(core, mine, across(other, 1))
    grad_input = (
        partial0.astype(F32)
        + from_pair.astype(F32)
        + from_mirror.astype(F32)
        + routed_input
    ).astype(BF16)
    return (grad_input, grads[1], grads[2], grads[0], g_gate[None], g_up[None], g_down[None])


def general_body(
    hidden_in,
    cotangent,
    routes,
    gate_values,
    dense_gate,
    dense_up,
    dense_down,
    expert_gate,
    expert_up,
    expert_down,
):
    experts = lax.axis_size("tp")
    me = lax.axis_index("tp")
    dispatch, weight = slot_tables(routes, gate_values, me, experts)
    sent = slots_to_send(hidden_in, cotangent, dispatch, weight, experts)
    got = exchange_slots(sent, me, experts)
    slots = lax.all_gather(got, "ep", axis=0, tiled=False)
    slot_rows, slot_cot = slots[:, 0].reshape(-1, hidden_in.shape[1]), slots[:, 1].reshape(
        -1, hidden_in.shape[1]
    )
    rows = lax.all_gather(hidden_in, "tp", axis=0, tiled=True)
    cots = lax.all_gather(cotangent, "tp", axis=0, tiled=True)
    down = lax.all_gather(dense_down, "ep", axis=1, tiled=True)
    act, grad_gate, grad_up, partial = plain_block(rows, cots, dense_gate, dense_up, down)
    dense_input = lax.psum_scatter(partial, "tp", scatter_dimension=0, tiled=True)
    grads = [
        lax.psum_scatter(
            lax.dot_general(a, b, LEADING, preferred_element_type=F32).astype(BF16),
            "ep",
            scatter_dimension=1,
            tiled=True,
        )
        for a, b in ((act, cots), (grad_gate, rows), (grad_up, rows))
    ]
    g_gate, g_up, g_down, slot_terms = expert_layer(
        slot_rows, slot_cot, expert_gate[0], expert_up[0], expert_down[0]
    )
    routed = lax.psum_scatter(slot_terms, "ep", scatter_dimension=0, tiled=True)
    routed_input = slots_back(routed, dispatch, me, experts)
    grad_input = (dense_input.astype(F32) + routed_input).astype(BF16)
    return (grad_input, grads[1], grads[2], grads[0], g_gate[None], g_up[None], g_down[None])


def solution(mesh):
    placed = (
        P(("ep", "tp"), None),
        P(("ep", "tp"), None),
        P(("ep", "tp"), None),
        P(("ep", "tp"), None),
        P("tp", None),
        P("tp", None),
        P("tp", "ep"),
        P("tp", "ep", None),
        P("tp", "ep", None),
        P("tp", "ep", None),
    )
    in_line = mesh.shape["tp"] == 4 and mesh.shape["ep"] == 8
    return jax.shard_map(
        line_body if in_line else general_body,
        mesh=mesh,
        in_specs=placed,
        out_specs=(
            P(("ep", "tp"), None),
            P("tp", "ep"),
            P("tp", "ep"),
            P("tp", "ep"),
            P("tp", "ep", None),
            P("tp", "ep", None),
            P("tp", "ep", None),
        ),
        check_vma=False,
    )
```

profile of v0, /device:TPU:0, one launch (start us, length us, event | category | flops | bytes accessed | tf_op | source)
XLA Modules:
  0.0 297.9 jit_solution(4518072647949655284)
XLA Ops:
  7.2 0.7 all-gather.4.cloned.1.call-update
  7.9 1.6 pad_maximum_fusion.refs_0_.refs_6_
  9.6 5.1 %collective-permute-start = (bf16[2,128,3584]{2,1,0:T(8,128)(2,1)S(1)}, bf16[2,128,3584]{2,1,0:T(8,128)(2,1)}, u32[]{:S(2)}, u32[]{:S(2)}) collective-permute-start(bf16[2,128,3584]{2,1,0:T(8,128)(2,1)S(1)} %pad_maximum_fusion.refs_0_.refs_6_), channel_id=1, source_target_pairs={{0,24},{8,16},{16,8},{24,0},{1,25},{9,17},{17,9},{25,1},{2,26},{10... | collective-permute-start | bytes 5505032 | tf_op jit(solution)/shard_map/ppermute | solution.py:360
  15.7 1.0 mul.34
  16.7 1.2 reduce-window.6
  18.9 1.0 eq.66
  20.0 1.2 fusion.5
  21.8 1.1 multiply_reduce_fusion
  23.0 1.4 fusion
  24.5 1.0 fusion.2
  25.5 3.4 %all-to-all-start = ((bf16[4,2,4,3584]{3,2,1,0:T(4,128)(2,1)}), bf16[4,2,4,3584]{3,2,1,0:T(4,128)(2,1)S(1)}, u32[]{:S(2)}, u32[]{:S(2)}) async-start(bf16[4,2,4,3584]{3,2,1,0:T(4,128)(2,1)} %fusion.2), calls=%async_computation | async-start | bytes 458752 | tf_op jit(solution)/shard_map/all_to_all | solution.py:56
  29.0 69.1 %all-to-all-done = bf16[4,2,4,3584]{3,2,1,0:T(4,128)(2,1)S(1)} async-done(((bf16[4,2,4,3584]{3,2,1,0:T(4,128)(2,1)}), bf16[4,2,4,3584]{3,2,1,0:T(4,128)(2,1)S(1)}, u32[]{:S(2)}, u32[]{:S(2)}) %all-to-all-start) | async-done | bytes 229408 | tf_op jit(solution)/shard_map/all_to_all | solution.py:56
  98.3 2.3 copy-done.1
  100.6 2.2 copy-done.4
  102.8 2.2 copy-done.7
  105.1 5.0 %dense_block.3 = (bf16[3,304,128]{2,1,0:T(8,128)(2,1)S(1)}, bf16[3,304,128]{2,1,0:T(8,128)(2,1)S(1)}, bf16[128,3584]{1,0:T(8,128)(2,1)S(1)}) custom-call(s32[1]{0:T(128)} %bitcast.2.core_ref, bf16[2,128,3584]{2,1,0:T(8,128)(2,1)S(1)} %pad_maximum_fusion.refs_0_.refs_6_, bf16[608,3584]{1,0:T(8,128)(2,1)S(1)} %copy-done.4, bf16[608,3584]{1,0:T(8,128)(2,1)S(1)} %copy-done.7, ...), custom_call_target="tpu_custom_call" | custom-call | flops 2789212160 | bytes 16293888 | tf_op jit(solution)/shard_map/dense_block/pallas_call | solution.py:153
  110.1 0.7 copy-done.11
  110.8 0.7 copy.47
  112.7 2.3 copy-done.2
  115.0 2.2 copy-done.5
  117.2 2.4 copy-done.8
  119.6 9.6 %dense_block.4 = (bf16[3,304,256]{2,1,0:T(8,128)(2,1)S(1)}, bf16[3,304,256]{2,1,0:T(8,128)(2,1)S(1)}, bf16[256,3584]{1,0:T(8,128)(2,1)S(1)}) custom-call(s32[1]{0:T(128)} %bitcast.2.core_ref, bf16[2,128,3584]{2,1,0:T(8,128)(2,1)} %collective-permute-done.1.refs_0_.refs_8_, bf16[2,128,3584]{2,1,0:T(8,128)(2,1)} %collective-permute-done.refs_1_.refs_9_, ...), custom_call_target="tpu_custom_call" | custom-call | flops 5578424320 | bytes 19513344 | tf_op jit(solution)/shard_map/dense_block/pallas_call | solution.py:153
  129.2 0.8 copy-done.10
  130.0 1.2 copy-done.13
  131.4 7.3 %all-gather.6.cloned.1.call-done = bf16[16,16,3584]{2,1,0:T(8,128)(2,1)} async-done(((bf16[2,16,3584]{2,1,0:T(8,128)(2,1)}), bf16[16,16,3584]{2,1,0:T(8,128)(2,1)}) %all-gather.6.cloned.1.call-update) | async-done | bytes 1835024 | tf_op jit(solution)/shard_map/all_gather | solution.py:381
  138.7 1.6 fusion.12
  140.6 2.2 copy-done.18
  142.8 2.2 copy-done.19
  145.1 2.2 copy-done.20
  147.3 16.1 %expert_block.1 = (bf16[608,3584]{1,0:T(8,128)(2,1)}, bf16[608,3584]{1,0:T(8,128)(2,1)}, bf16[608,3584]{1,0:T(8,128)(2,1)}, bf16[128,3584]{1,0:T(8,128)(2,1)}) custom-call(bf16[128,3584]{1,0:T(8,128)(2,1)S(1)} %bitcast.51, bf16[128,3584]{1,0:T(8,128)(2,1)S(1)} %bitcast.50, bf16[608,3584]{1,0:T(8,128)(2,1)S(1)} %bitcast.52, bf16[608,3584]{1,0:T(8,128)(2,1)S(1)} %bitcast.53, ...), custom_call_target="tpu_custom_call" | custom-call | flops 4462739456 | bytes 28901376 | tf_op jit(solution)/shard_map/expert_block/pallas_call | solution.py:206
  164.5 2.3 copy-done.3
  166.8 2.2 copy-done.6
  169.0 2.3 copy-done.9
  171.3 7.6 %dense_block.5 = (bf16[3,304,128]{2,1,0:T(8,128)(2,1)S(1)}, bf16[3,304,128]{2,1,0:T(8,128)(2,1)S(1)}, bf16[128,3584]{1,0:T(8,128)(2,1)}) custom-call(s32[1]{0:T(128)} %bitcast.2.core_ref, bf16[2,128,3584]{2,1,0:T(8,128)(2,1)} %collective-permute-done.2.refs_0_.refs_12_, bf16[608,3584]{1,0:T(8,128)(2,1)S(1)} %copy-done.6, bf16[608,3584]{1,0:T(8,128)(2,1)S(1)} %copy-done.9, ...), custom_call_target="tpu_custom_call" | custom-call | flops 2789212160 | bytes 16293888 | tf_op jit(solution)/shard_map/dense_block/pallas_call | solution.py:153
  178.9 0.7 copy-done.12
  179.6 1.5 collective-permute-start.12
  181.1 1.0 split.6
  182.7 0.7 copy-done.22
  183.4 6.1 %weight_terms.4 = (bf16[3,160,896]{2,1,0:T(8,128)(2,1)}, bf16[3,144,896]{2,1,0:T(8,128)(2,1)}) custom-call(s32[1]{0:T(128)} %bitcast.10.tile_ref, bf16[3,304,128]{2,1,0:T(8,128)(2,1)} %copy-done.11, bf16[3,304,128]{2,1,0:T(8,128)(2,1)} %copy-done.21, bf16[3,304,256]{2,1,0:T(8,128)(2,1)} %copy-done.10, bf16[3,304,256]{2,1,0:T(8,128)(2,1)} %collective-permute-done.5.refs_3_, ...), custom_call_target="tpu_custom_call" | custom-call | flops 1673527296 | bytes 7172096 | tf_op jit(solution)/shard_map/weight_terms/pallas_call | solution.py:308
  189.5 1.4 collective-permute-start.10
  191.2 5.9 %weight_terms.6 = (bf16[3,160,896]{2,1,0:T(8,128)(2,1)}, bf16[3,144,896]{2,1,0:T(8,128)(2,1)}) custom-call(s32[1]{0:T(128)} %bitcast.18.tile_ref, bf16[3,304,128]{2,1,0:T(8,128)(2,1)} %copy-done.11, bf16[3,304,128]{2,1,0:T(8,128)(2,1)} %copy-done.21, bf16[3,304,256]{2,1,0:T(8,128)(2,1)} %copy-done.10, bf16[3,304,256]{2,1,0:T(8,128)(2,1)} %collective-permute-done.5.refs_3_, ...), custom_call_target="tpu_custom_call" | custom-call | flops 1673527296 | bytes 7172096 | tf_op jit(solution)/shard_map/weight_terms/pallas_call | solution.py:308
  197.1 6.0 %collective-permute-done.12 = bf16[128,3584]{1,0:T(8,128)(2,1)} collective-permute-done((bf16[128,3584]{1,0:T(8,128)(2,1)}, bf16[128,3584]{1,0:T(8,128)(2,1)}, u32[]{:S(2)}, u32[]{:S(2)}) %collective-permute-start.12) | collective-permute-done | bytes 917536 | tf_op jit(solution)/shard_map/ppermute | solution.py:357
  203.1 2.3 add_convert_fusion.1
  205.4 3.3 %collective-permute-start.16 = (bf16[128,3584]{1,0:T(8,128)(2,1)}, bf16[128,3584]{1,0:T(8,128)(2,1)}, u32[]{:S(2)}, u32[]{:S(2)}) collective-permute-start(bf16[128,3584]{1,0:T(8,128)(2,1)} %add_convert_fusion.1), channel_id=1, source_target_pairs={{0,24},{8,16},{16,8},{24,0},{1,25},{9,17},{17,9},{25,1},{2,26},{10... | collective-permute-start | bytes 2752520 | tf_op jit(solution)/shard_map/ppermute | solution.py:360
  208.7 0.9 reshape.122
  209.7 0.7 constant_dynamic-slice_fusion
  210.4 5.9 %weight_terms.5 = (bf16[3,160,896]{2,1,0:T(8,128)(2,1)}, bf16[3,144,896]{2,1,0:T(8,128)(2,1)}) custom-call(s32[1]{0:T(128)} %bitcast.17.tile_ref, bf16[3,304,128]{2,1,0:T(8,128)(2,1)} %copy-done.11, bf16[3,304,128]{2,1,0:T(8,128)(2,1)} %copy-done.21, bf16[3,304,256]{2,1,0:T(8,128)(2,1)} %copy-done.10, bf16[3,304,256]{2,1,0:T(8,128)(2,1)} %collective-permute-done.5.refs_3_, ...), custom_call_target="tpu_custom_call" | custom-call | flops 1673527296 | bytes 7172096 | tf_op jit(solution)/shard_map/weight_terms/pallas_call | solution.py:308
  216.2 6.0 %weight_terms.7 = (bf16[3,160,896]{2,1,0:T(8,128)(2,1)}, bf16[3,144,896]{2,1,0:T(8,128)(2,1)}) custom-call(s32[1]{0:T(128)} %bitcast.19.tile_ref, bf16[3,304,128]{2,1,0:T(8,128)(2,1)} %copy-done.11, bf16[3,304,128]{2,1,0:T(8,128)(2,1)} %copy-done.21, bf16[3,304,256]{2,1,0:T(8,128)(2,1)} %copy-done.10, bf16[3,304,256]{2,1,0:T(8,128)(2,1)} %collective-permute-done.5.refs_3_, ...), custom_call_target="tpu_custom_call" | custom-call | flops 1673527296 | bytes 7172096 | tf_op jit(solution)/shard_map/weight_terms/pallas_call | solution.py:308
  222.2 1.1 collective-permute-start.18
  223.4 3.1 %collective-permute-start.17 = (bf16[4,3584]{1,0:T(4,128)(2,1)}, bf16[4,3584]{1,0:T(4,128)(2,1)S(1)}, u32[]{:S(2)}, u32[]{:S(2)}) collective-permute-start(bf16[4,3584]{1,0:T(4,128)(2,1)} %get-tuple-element.132), channel_id=1, source_target_pairs={{0,24},{8,0},{16,8},{24,16},{1,25},{9,1},{17,9},{25,17},{2,26},{10... | collective-permute-start | bytes 86024 | tf_op jit(solution)/shard_map/ppermute | solution.py:40
  226.4 2.3 add_convert_fusion.2
  228.7 1.5 collective-permute-start.20
  230.2 14.7 %collective-permute-done.19 = bf16[4,3584]{1,0:T(4,128)(2,1)S(1)} collective-permute-done((bf16[4,3584]{1,0:T(4,128)(2,1)S(1)}, bf16[4,3584]{1,0:T(4,128)(2,1)S(1)}, u32[]{:S(2)}, u32[]{:S(2)}) %collective-permute-start.19) | collective-permute-done | bytes 28704 | tf_op jit(solution)/shard_map/ppermute | solution.py:40
  244.9 1.4 collective-permute-start.13
  246.3 2.4 add_convert_fusion.3
  248.7 0.7 collective-permute-done.18
  249.4 1.5 collective-permute-start.14
  252.1 1.3 fusion.13
  253.4 13.4 %collective-permute-done.14.refs_5_ = bf16[3,144,896]{2,1,0:T(8,128)(2,1)} collective-permute-done((bf16[3,144,896]{2,1,0:T(8,128)(2,1)}, bf16[3,144,896]{2,1,0:T(8,128)(2,1)}, u32[]{:S(2)}, u32[]{:S(2)}) %collective-permute-start.14) | collective-permute-done | bytes 774176 | tf_op jit(solution)/shard_map/ppermute | solution.py:363
  267.2 14.5 %collective-permute-done.21.refs_4_ = bf16[3,144,896]{2,1,0:T(8,128)(2,1)} collective-permute-done((bf16[3,144,896]{2,1,0:T(8,128)(2,1)}, bf16[3,144,896]{2,1,0:T(8,128)(2,1)}, u32[]{:S(2)}, u32[]{:S(2)}) %collective-permute-start.21) | collective-permute-done | bytes 774176 | tf_op jit(solution)/shard_map/ppermute | solution.py:363
  281.8 2.7 final_sum.1
  284.5 3.0 %add_convert_fusion = bf16[128,3584]{1,0:T(8,128)(2,1)} fusion(f32[128,3584]{1,0:T(8,128)S(1)} %fusion.13, bf16[128,3584]{1,0:T(8,128)(2,1)} %collective-permute-done.16, bf16[128,3584]{1,0:T(8,128)(2,1)} %collective-permute-done.15, bf16[128,3584]{1,0:T(8,128)(2,1)S(1)} %get-tuple-element.68), kind=kLoop, calls=%fused_computation.4 | loop fusion | flops 3211264 | bytes 5505024 | tf_op jit(solution)/shard_map/convert_element_type | solution.py:428
  287.5 1.0 copy-done.24
  288.5 2.9 join_halves.1
  (115 shorter events, 8.4 us)
Async XLA Ops:
  7.2 91.1 %all-gather.4.cloned.1.call-start = ((), (), s32[]{:S(2)}) async-start(), calls=%async_computation.2 | async-start | bytes 5160960 | tf_op jit(solution)/shard_map/all_gather | solution.py:354
  7.9 6.8 %copy-start.31 = (s32[128,2]{0,1:T(2,128)S(1)}, s32[128,2]{0,1:T(2,128)}, u32[]{:S(2)}) copy-start(s32[128,2]{0,1:T(2,128)} %param.12) | copy-start | bytes 3076
  9.5 102.2 %copy-start = (bf16[2,128,3584]{2,1,0:T(8,128)(2,1)}, bf16[2,128,3584]{2,1,0:T(8,128)(2,1)S(1)}, u32[]{:S(2)}) copy-start(bf16[2,128,3584]{2,1,0:T(8,128)(2,1)S(1)} %pad_maximum_fusion.refs_0_.refs_6_) | copy-start | bytes 5505028
  9.6 11.7 %copy-start.23 = (bf16[128,3584]{1,0:T(8,128)(2,1)S(1)}, bf16[128,3584]{1,0:T(8,128)(2,1)}, u32[]{:S(2)}) copy-start(bf16[128,3584]{1,0:T(8,128)(2,1)} %param.10) | copy-start | bytes 2752516
  9.6 101.2 %collective-permute-start = (bf16[2,128,3584]{2,1,0:T(8,128)(2,1)S(1)}, bf16[2,128,3584]{2,1,0:T(8,128)(2,1)}, u32[]{:S(2)}, u32[]{:S(2)}) collective-permute-start(bf16[2,128,3584]{2,1,0:T(8,128)(2,1)S(1)} %pad_maximum_fusion.refs_0_.refs_6_), channel_id=1, source_target_pairs={{0,24},{8,16},{16,8},{24,0},{1,25},{9,17},{17,9},{25,1},{2,26},{10... | collective-permute-start | bytes 5505032 | tf_op jit(solution)/shard_map/ppermute | solution.py:360
  14.7 96.1 %collective-permute-start.1 = (bf16[2,128,3584]{2,1,0:T(8,128)(2,1)S(1)}, bf16[2,128,3584]{2,1,0:T(8,128)(2,1)}, u32[]{:S(2)}, u32[]{:S(2)}) collective-permute-start(bf16[2,128,3584]{2,1,0:T(8,128)(2,1)S(1)} %pad_maximum_fusion.refs_0_.refs_6_), channel_id=1, source_target_pairs={{0,8},{8,0},{16,24},{24,16},{1,9},{9,1},{17,25},{25,17},{2,10},{10... | collective-permute-start | bytes 5505032 | tf_op jit(solution)/shard_map/ppermute | solution.py:357
  15.7 5.9 %copy-start.32 = (f32[128,2]{0,1:T(2,128)S(1)}, f32[128,2]{0,1:T(2,128)}, u32[]{:S(2)}) copy-start(f32[128,2]{0,1:T(2,128)} %param.13) | copy-start | bytes 3076
  21.2 4.4 %copy-start.28 = (bf16[128,16]{1,0:T(8,128)(2,1)}, bf16[128,16]{1,0:T(8,128)(2,1)S(1)}, u32[]{:S(2)}) copy-start(bf16[128,16]{1,0:T(8,128)(2,1)S(1)} %fusion.5) | copy-start | bytes 12292
  25.5 72.5 %all-to-all-start = ((bf16[4,2,4,3584]{3,2,1,0:T(4,128)(2,1)}), bf16[4,2,4,3584]{3,2,1,0:T(4,128)(2,1)S(1)}, u32[]{:S(2)}, u32[]{:S(2)}) async-start(bf16[4,2,4,3584]{3,2,1,0:T(4,128)(2,1)} %fusion.2), calls=%async_computation | async-start | bytes 458752 | tf_op jit(solution)/shard_map/all_to_all | solution.py:56
  28.9 109.7 %all-gather.6.cloned.1.call-start = ((), (), s32[]{:S(2)}) async-start(), calls=%async_computation.4 | async-start | bytes 2064384 | tf_op jit(solution)/shard_map/all_gather | solution.py:381
  98.3 2.3 copy-start.1
  100.6 2.2 copy-start.4
  102.8 2.2 copy-start.7
  110.1 0.7 copy-start.11
  111.5 91.6 %reduce-scatter.2.cloned.1.call-start = ((), (), s32[]{:S(2)}) async-start(), calls=%async_computation.3 | async-start | bytes 1032192 | tf_op jit(solution)/shard_map/reduce_scatter | solution.py:392
  111.7 28.5 %collective-permute-start.4 = (bf16[2,128,3584]{2,1,0:T(8,128)(2,1)S(1)}, bf16[2,128,3584]{2,1,0:T(8,128)(2,1)}, u32[]{:S(2)}, u32[]{:S(2)}) collective-permute-start(bf16[2,128,3584]{2,1,0:T(8,128)(2,1)S(1)} %pad_maximum_fusion.refs_0_.refs_6_), channel_id=1, source_target_pairs={{0,1},{1,0},{2,3},{3,2},{4,5},{5,4},{6,7},{7,6},{8,9},{9,8},{10,11... | collective-permute-start | bytes 5505032 | tf_op jit(solution)/shard_map/ppermute | solution.py:363
  111.8 52.3 %collective-permute-start.2 = (bf16[2,128,3584]{2,1,0:T(8,128)(2,1)}, bf16[2,128,3584]{2,1,0:T(8,128)(2,1)}, u32[]{:S(2)}, u32[]{:S(2)}) collective-permute-start(bf16[2,128,3584]{2,1,0:T(8,128)(2,1)} %collective-permute-done.refs_1_.refs_9_), channel_id=1, source_target_pairs={{0,8},{8,0},{16,24},{24,16},{1,9},{9,1},{17,25},{25,17},{2,10},{10... | collective-permute-start | bytes 5505032 | tf_op jit(solution)/shard_map/ppermute | solution.py:357
  112.2 52.0 %collective-permute-start.7 = (bf16[2,128,3584]{2,1,0:T(8,128)(2,1)}, bf16[2,128,3584]{2,1,0:T(8,128)(2,1)}, u32[]{:S(2)}, u32[]{:S(2)}) collective-permute-start(bf16[2,128,3584]{2,1,0:T(8,128)(2,1)} %collective-permute-done.refs_1_.refs_9_), channel_id=1, source_target_pairs={{0,1},{1,0},{2,3},{3,2},{4,5},{5,4},{6,7},{7,6},{8,9},{9,8},{10,11... | collective-permute-start | bytes 5505032 | tf_op jit(solution)/shard_map/ppermute | solution.py:363
  112.3 51.8 %collective-permute-start.6 = (bf16[2,128,3584]{2,1,0:T(8,128)(2,1)}, bf16[2,128,3584]{2,1,0:T(8,128)(2,1)}, u32[]{:S(2)}, u32[]{:S(2)}) collective-permute-start(bf16[2,128,3584]{2,1,0:T(8,128)(2,1)} %collective-permute-done.1.refs_0_.refs_8_), channel_id=1, source_target_pairs={{0,1},{1,0},{2,3},{3,2},{4,5},{5,4},{6,7},{7,6},{8,9},{9,8},{10,11... | collective-permute-start | bytes 5505032 | tf_op jit(solution)/shard_map/ppermute | solution.py:363
  112.7 2.3 copy-start.2
  115.0 2.2 copy-start.5
  117.2 2.4 copy-start.8
  129.2 0.8 copy-start.10
  130.0 1.3 copy-start.13
  131.2 32.2 %collective-permute-start.5 = (bf16[3,304,256]{2,1,0:T(8,128)(2,1)S(1)}, bf16[3,304,256]{2,1,0:T(8,128)(2,1)}, u32[]{:S(2)}, u32[]{:S(2)}) collective-permute-start(bf16[3,304,256]{2,1,0:T(8,128)(2,1)S(1)} %get-tuple-element.78), channel_id=1, source_target_pairs={{0,1},{1,0},{2,3},{3,2},{4,5},{5,4},{6,7},{7,6},{8,9},{9,8},{10,11... | collective-permute-start | bytes 1400840 | tf_op jit(solution)/shard_map/ppermute | solution.py:363
  140.3 23.1 %collective-permute-start.3 = (bf16[3,304,128]{2,1,0:T(8,128)(2,1)S(1)}, bf16[3,304,128]{2,1,0:T(8,128)(2,1)S(1)}, u32[]{:S(2)}, u32[]{:S(2)}) collective-permute-start(bf16[3,304,128]{2,1,0:T(8,128)(2,1)S(1)} %get-tuple-element.76), channel_id=1, source_target_pairs={{0,1},{1,0},{2,3},{3,2},{4,5},{5,4},{6,7},{7,6},{8,9},{9,8},{10,11... | collective-permute-start | bytes 700424 | tf_op jit(solution)/shard_map/ppermute | solution.py:363
  140.6 2.2 copy-start.18
  142.8 2.2 copy-start.19
  145.1 2.2 copy-start.20
  163.4 0.7 copy-start.21
  164.1 18.6 %collective-permute-start.9 = (bf16[2,128,3584]{2,1,0:T(8,128)(2,1)}, bf16[2,128,3584]{2,1,0:T(8,128)(2,1)}, u32[]{:S(2)}, u32[]{:S(2)}) collective-permute-start(bf16[2,128,3584]{2,1,0:T(8,128)(2,1)} %collective-permute-done.2.refs_0_.refs_12_), channel_id=1, source_target_pairs={{0,1},{1,0},{2,3},{3,2},{4,5},{5,4},{6,7},{7,6},{8,9},{9,8},{10,11... | collective-permute-start | bytes 5505032 | tf_op jit(solution)/shard_map/ppermute | solution.py:363
  164.5 2.3 copy-start.3
  166.8 2.2 copy-start.6
  169.0 2.3 copy-start.9
  171.3 9.8 %copy-start.14 = (bf16[256,3584]{1,0:T(8,128)(2,1)S(1)}, bf16[256,3584]{1,0:T(8,128)(2,1)}, u32[]{:S(2)}) copy-start(bf16[256,3584]{1,0:T(8,128)(2,1)} %copy-done.13) | copy-start | bytes 5505028
  178.9 0.7 copy-start.12
  179.6 23.5 %collective-permute-start.12 = (bf16[128,3584]{1,0:T(8,128)(2,1)}, bf16[128,3584]{1,0:T(8,128)(2,1)}, u32[]{:S(2)}, u32[]{:S(2)}) collective-permute-start(bf16[128,3584]{1,0:T(8,128)(2,1)} %get-tuple-element.98), channel_id=1, source_target_pairs={{0,8},{8,0},{16,24},{24,16},{1,9},{9,1},{17,25},{25,17},{2,10},{10... | collective-permute-start | bytes 2752520 | tf_op jit(solution)/shard_map/ppermute | solution.py:357
  181.1 1.5 collective-permute-start.8
  182.2 46.5 %collective-permute-start.15 = (bf16[128,3584]{1,0:T(8,128)(2,1)}, bf16[128,3584]{1,0:T(8,128)(2,1)}, u32[]{:S(2)}, u32[]{:S(2)}) collective-permute-start(bf16[128,3584]{1,0:T(8,128)(2,1)} %split.6), channel_id=1, source_target_pairs={{0,8},{8,0},{16,24},{24,16},{1,9},{9,1},{17,25},{25,17},{2,10},{10... | collective-permute-start | bytes 2752520 | tf_op jit(solution)/shard_map/ppermute | solution.py:357
  182.7 0.7 copy-start.22
  189.5 33.9 %collective-permute-start.10 = (bf16[3,160,896]{2,1,0:T(8,128)(2,1)}, bf16[3,160,896]{2,1,0:T(8,128)(2,1)}, u32[]{:S(2)}, u32[]{:S(2)}) collective-permute-start(bf16[3,160,896]{2,1,0:T(8,128)(2,1)} %get-tuple-element.96), channel_id=1, source_target_pairs={{0,2},{1,3},{2,0},{3,1},{4,6},{5,7},{6,4},{7,5},{8,10},{9,11},{10,... | collective-permute-start | bytes 2580488 | tf_op jit(solution)/shard_map/ppermute | solution.py:363
  190.9 31.3 %collective-permute-start.11 = (bf16[3,144,896]{2,1,0:T(8,128)(2,1)}, bf16[3,144,896]{2,1,0:T(8,128)(2,1)S(1)}, u32[]{:S(2)}, u32[]{:S(2)}) collective-permute-start(bf16[3,144,896]{2,1,0:T(8,128)(2,1)} %get-tuple-element.97), channel_id=1, source_target_pairs={{0,4},{1,5},{2,6},{3,7},{4,0},{5,1},{6,2},{7,3},{8,12},{9,13},{10,... | collective-permute-start | bytes 2322440 | tf_op jit(solution)/shard_map/ppermute | solution.py:363
  205.4 48.0 %collective-permute-start.16 = (bf16[128,3584]{1,0:T(8,128)(2,1)}, bf16[128,3584]{1,0:T(8,128)(2,1)}, u32[]{:S(2)}, u32[]{:S(2)}) collective-permute-start(bf16[128,3584]{1,0:T(8,128)(2,1)} %add_convert_fusion.1), channel_id=1, source_target_pairs={{0,24},{8,16},{16,8},{24,0},{1,25},{9,17},{17,9},{25,1},{2,26},{10... | collective-permute-start | bytes 2752520 | tf_op jit(solution)/shard_map/ppermute | solution.py:360
  210.4 34.5 %collective-permute-start.19 = (bf16[4,3584]{1,0:T(4,128)(2,1)S(1)}, bf16[4,3584]{1,0:T(4,128)(2,1)S(1)}, u32[]{:S(2)}, u32[]{:S(2)}) collective-permute-start(bf16[4,3584]{1,0:T(4,128)(2,1)S(1)} %get-tuple-element.130), channel_id=1, source_target_pairs={{0,8},{8,16},{16,24},{24,0},{1,9},{9,17},{17,25},{25,1},{2,10},{10... | collective-permute-start | bytes 86024 | tf_op jit(solution)/shard_map/ppermute | solution.py:40
  216.2 10.2 %copy-start.25 = (bf16[3,160,896]{2,1,0:T(8,128)(2,1)S(1)}, bf16[3,160,896]{2,1,0:T(8,128)(2,1)}, u32[]{:S(2)}) copy-start(bf16[3,160,896]{2,1,0:T(8,128)(2,1)} %get-tuple-element.95) | copy-start | bytes 2580484
  222.2 24.1 %copy-start.27 = (bf16[3,144,896]{2,1,0:T(8,128)(2,1)S(1)}, bf16[3,144,896]{2,1,0:T(8,128)(2,1)}, u32[]{:S(2)}) copy-start(bf16[3,144,896]{2,1,0:T(8,128)(2,1)} %get-tuple-element.105) | copy-start | bytes 2322436
  222.2 24.0 %copy-start.26 = (bf16[3,144,896]{2,1,0:T(8,128)(2,1)}, bf16[3,144,896]{2,1,0:T(8,128)(2,1)S(1)}, u32[]{:S(2)}) copy-start(bf16[3,144,896]{2,1,0:T(8,128)(2,1)S(1)} %collective-permute-done.11) | copy-start | bytes 2322436
  222.2 27.2 %collective-permute-start.18 = (bf16[4,3584]{1,0:T(4,128)(2,1)}, bf16[4,3584]{1,0:T(4,128)(2,1)S(1)}, u32[]{:S(2)}, u32[]{:S(2)}) collective-permute-start(bf16[4,3584]{1,0:T(4,128)(2,1)} %get-tuple-element.131), channel_id=1, source_target_pairs={{0,16},{8,24},{16,0},{24,8},{1,17},{9,25},{17,1},{25,9},{2,18},{10... | collective-permute-start | bytes 86024 | tf_op jit(solution)/shard_map/ppermute | solution.py:40
  223.4 27.5 %collective-permute-start.17 = (bf16[4,3584]{1,0:T(4,128)(2,1)}, bf16[4,3584]{1,0:T(4,128)(2,1)S(1)}, u32[]{:S(2)}, u32[]{:S(2)}) collective-permute-start(bf16[4,3584]{1,0:T(4,128)(2,1)} %get-tuple-element.132), channel_id=1, source_target_pairs={{0,24},{8,0},{16,8},{24,16},{1,25},{9,1},{17,9},{25,17},{2,26},{10... | collective-permute-start | bytes 86024 | tf_op jit(solution)/shard_map/ppermute | solution.py:40
  228.7 53.0 %collective-permute-start.20 = (bf16[3,160,896]{2,1,0:T(8,128)(2,1)}, bf16[3,160,896]{2,1,0:T(8,128)(2,1)S(1)}, u32[]{:S(2)}, u32[]{:S(2)}) collective-permute-start(bf16[3,160,896]{2,1,0:T(8,128)(2,1)} %get-tuple-element.114), channel_id=1, source_target_pairs={{0,2},{1,3},{2,0},{3,1},{4,6},{5,7},{6,4},{7,5},{8,10},{9,11},{10,... | collective-permute-start | bytes 2580488 | tf_op jit(solution)/shard_map/ppermute | solution.py:363
  244.9 1.4 copy-start.29
  244.9 22.4 %collective-permute-start.13 = (bf16[3,160,896]{2,1,0:T(8,128)(2,1)}, bf16[3,160,896]{2,1,0:T(8,128)(2,1)}, u32[]{:S(2)}, u32[]{:S(2)}) collective-permute-start(bf16[3,160,896]{2,1,0:T(8,128)(2,1)} %add_convert_fusion.2), channel_id=1, source_target_pairs={{0,4},{1,5},{2,6},{3,7},{4,0},{5,1},{6,2},{7,3},{8,12},{9,13},{10,... | collective-permute-start | bytes 2580488 | tf_op jit(solution)/shard_map/ppermute | solution.py:363
  246.2 5.1 %copy-start.30 = (bf16[4,3584]{1,0:T(4,128)(2,1)S(1)}, bf16[4,3584]{1,0:T(4,128)(2,1)}, u32[]{:S(2)}) copy-start(bf16[4,3584]{1,0:T(4,128)(2,1)} %copy-done.29) | copy-start | bytes 86020
  246.3 35.5 %copy-start.16 = (bf16[3,160,896]{2,1,0:T(8,128)(2,1)S(1)}, bf16[3,160,896]{2,1,0:T(8,128)(2,1)}, u32[]{:S(2)}) copy-start(bf16[3,160,896]{2,1,0:T(8,128)(2,1)} %get-tuple-element.113.refs_0_) | copy-start | bytes 2580484
  246.3 35.5 %copy-start.17 = (bf16[3,144,896]{2,1,0:T(8,128)(2,1)S(1)}, bf16[3,144,896]{2,1,0:T(8,128)(2,1)}, u32[]{:S(2)}) copy-start(bf16[3,144,896]{2,1,0:T(8,128)(2,1)} %get-tuple-element.116.refs_3_) | copy-start | bytes 2322436
  249.4 17.4 %collective-permute-start.14 = (bf16[3,144,896]{2,1,0:T(8,128)(2,1)}, bf16[3,144,896]{2,1,0:T(8,128)(2,1)}, u32[]{:S(2)}, u32[]{:S(2)}) collective-permute-start(bf16[3,144,896]{2,1,0:T(8,128)(2,1)} %add_convert_fusion.3), channel_id=1, source_target_pairs={{0,2},{1,3},{2,0},{3,1},{4,6},{5,7},{6,4},{7,5},{8,10},{9,11},{10,... | collective-permute-start | bytes 2322440 | tf_op jit(solution)/shard_map/ppermute | solution.py:363
  250.9 30.8 %collective-permute-start.21 = (bf16[3,144,896]{2,1,0:T(8,128)(2,1)}, bf16[3,144,896]{2,1,0:T(8,128)(2,1)}, u32[]{:S(2)}, u32[]{:S(2)}) collective-permute-start(bf16[3,144,896]{2,1,0:T(8,128)(2,1)} %get-tuple-element.117), channel_id=1, source_target_pairs={{0,4},{1,5},{2,6},{3,7},{4,0},{5,1},{6,2},{7,3},{8,12},{9,13},{10,... | collective-permute-start | bytes 2322440 | tf_op jit(solution)/shard_map/ppermute | solution.py:363
  284.4 3.1 %copy-start.15 = (bf16[3,304,448]{2,1,0:T(8,128)(2,1)}, bf16[3,304,448]{2,1,0:T(8,128)(2,1)S(1)}, u32[]{:S(2)}) copy-start(bf16[3,304,448]{2,1,0:T(8,128)(2,1)S(1)} %get-tuple-element.119.mine) | copy-start | bytes 2451460
  284.4 3.1 %collective-permute-start.22 = (bf16[3,304,448]{2,1,0:T(8,128)(2,1)S(1)}, bf16[3,304,448]{2,1,0:T(8,128)(2,1)S(1)}, u32[]{:S(2)}, u32[]{:S(2)}) collective-permute-start(bf16[3,304,448]{2,1,0:T(8,128)(2,1)S(1)} %get-tuple-element.120), channel_id=1, source_target_pairs={{0,1},{1,0},{2,3},{3,2},{4,5},{5,4},{6,7},{7,6},{8,9},{9,8},{10,11... | collective-permute-start | bytes 2451464 | tf_op jit(solution)/shard_map/ppermute | solution.py:363
  287.5 1.0 copy-start.24
Sparse Core Ops, SparseCore 0:
  9.9 41.0 all-gather.3
  111.6 27.0 all-gather.5
  164.6 36.6 reduce-scatter.1
where the time goes:
time: 300 us; the launch traced here: 298 us
  waiting for transfers between devices  127 us (42%)
  Pallas kernels  67.6 us (23%)
  local copies, waits for them, and re-layouts  42.9 us (14%)
  starting transfers between devices  26.7 us (9%)
  other arithmetic  16.7 us (6%)
  between operations  14.1 us (5%)
    all_to_all x1, waiting for transfers between devices, exchange_slots(): got = lax.all_to_all(sent, 'tp', split_axis=0, concat_axis=0, tiled=True)  69.1 us
    unnamed x68, local copies, waits for them, and re-layouts  33.2 us
    ppermute x14, waiting for transfers between devices, across(): return lax.ppermute(value, 'ep', [(i, i ^ apart) for i in range(8)])  28.3 us
    pallas_call x4, Pallas kernels, weight_terms(): pl.pallas_call(kernel, grid_spec=pltpu.PrefetchScalarGridSpec(num_scalar_...  23.8 us
    pallas_call x3, Pallas kernels, dense_block(): pl.pallas_call(kernel, in_specs=[pl.BlockSpec(memory_space=pltpu.SMEM)] +...  22.2 us
    pallas_call x1, Pallas kernels, expert_block(): pl.pallas_call(kernel, in_specs=[vmem] * 5, out_specs=[hbm, hbm, hbm, vme...  16.1 us
    ppermute x3, waiting for transfers between devices, shift(): return lax.ppermute(x, axis, [(i, (i + by) % size) for i in range(size)])  15.4 us
    ppermute x2, starting transfers between devices, mirror(): return lax.ppermute(value, 'tp', [(0, 3), (1, 2), (2, 1), (3, 0)])  8.42 us
  transfers between devices with their start and end apart: 27, of which 8 were waited for; matrix products, arithmetic and copies ran while one was open for 10% of the time, Pallas kernels for 21%

commit v1 on v0

--- a/solution.py
+++ b/solution.py
@@ -97,7 +97,7 @@
     return act, grad_gate, grad_up, partial.astype(BF16)
 
 
-VMEM_LIMIT = 24 * 1024 * 1024
+VMEM_LIMIT = 20 * 1024 * 1024
 VMEM_ALL = 60 * 1024 * 1024
 
 
@@ -173,7 +173,7 @@
 def expert_block(rows, cots, gate, up, down):
     tok, width = rows.shape
     units = gate.shape[0]
-    col = width // 4
+    col = 512
 
     def kernel(
         rows, cots, gate, up, down, g_gate, g_up, g_down, partial, turned, made, out_sems
@@ -224,19 +224,17 @@
 
 
 def final_sum(core, lows, highs):
-    count = len(lows)
-    _, cut, width = lows[0].shape
-    units = cut + highs[0].shape[1]
+    cut, width = lows[2].shape[1:]
+    units = cut + highs[2].shape[1]
     half = width // 2
 
     def kernel(core_ref, *refs):
         ins, (mine, other) = refs[:-2], refs[-2:]
         own_first = core_ref[0] == 0
         for i in range(3):
-            for begin, group in ((0, ins[:count]), (cut, ins[count:])):
-                total = group[0][i].astype(F32)
-                for ref in group[1:]:
-                    total = total + ref[i].astype(F32)
+            for begin, (own, near, far) in ((0, ins[:3]), (cut, ins[3:])):
+                total = own[i, :, width:].astype(F32) + near[i, :, width:].astype(F32)
+                total = total + far[i].astype(F32)
                 left, right = total[:, :half].astype(BF16), total[:, half:].astype(BF16)
                 size = total.shape[0]
                 mine[i, begin : begin + size] = jnp.where(own_first, left, right)
@@ -246,13 +244,13 @@
     shape = jax.ShapeDtypeStruct((3, units, half), BF16)
     return pl.pallas_call(
         kernel,
-        in_specs=[pl.BlockSpec(memory_space=pltpu.SMEM)] + [vmem] * (2 * count),
+        in_specs=[pl.BlockSpec(memory_space=pltpu.SMEM)] + [vmem] * 6,
         out_specs=[vmem, vmem],
         out_shape=[shape, shape],
         compiler_params=pltpu.CompilerParams(vmem_limit_bytes=VMEM_LIMIT),
         cost_estimate=pl.CostEstimate(
-            flops=3 * count * units * width,
-            bytes_accessed=6 * (count + 1) * units * width,
+            flops=9 * units * width,
+            bytes_accessed=24 * units * width,
             transcendentals=0,
         ),
         name="final_sum",
@@ -284,47 +282,44 @@
     return [grad.T for grad in grads]
 
 
-def weight_terms(tile, acts, blocks, width, cut):
+def weight_terms(tiles, acts, blocks, width, begin, end):
     units = acts[0].shape[1]
     tokens = sum(b.shape[1] for b in blocks)
+    size = end - begin
 
     def kernel(tile_ref, *refs):
-        a, b = refs[: len(acts)], refs[len(acts) : -2]
-        low, high = refs[-2:]
+        a, b, out = refs[: len(acts)], refs[len(acts) : -1], refs[-1]
         rows = jnp.concatenate([ref[0] for ref in b], axis=0)
         cots = jnp.concatenate([ref[1] for ref in b], axis=0)
         for i in range(3):
-            left = jnp.concatenate([ref[i] for ref in a], axis=1)
-            made = jnp.dot(left, cots if i == 0 else rows, preferred_element_type=F32).astype(BF16)
-            low[i] = made[:cut]
-            high[i] = made[cut:]
+            left = jnp.concatenate([ref[i, begin:end] for ref in a], axis=1)
+            out[i] = jnp.dot(
+                left, cots if i == 0 else rows, preferred_element_type=F32
+            ).astype(BF16)
 
     def whole(shape):
-        return pl.BlockSpec(shape, lambda i, tile_ref: (0, 0, 0))
+        return pl.BlockSpec(shape, lambda j, tile_ref: (0, 0, 0))
 
     def columns(block):
-        return pl.BlockSpec((*block.shape[:2], width), lambda i, tile_ref: (0, 0, tile_ref[0]))
+        return pl.BlockSpec((*block.shape[:2], width), lambda j, tile_ref: (0, 0, tile_ref[j]))
 
     return pl.pallas_call(
         kernel,
         grid_spec=pltpu.PrefetchScalarGridSpec(
             num_scalar_prefetch=1,
-            grid=(1,),
+            grid=(2,),
             in_specs=[whole(a.shape) for a in acts] + [columns(b) for b in blocks],
-            out_specs=[whole((3, cut, width)), whole((3, units - cut, width))],
-        ),
-        out_shape=[
-            jax.ShapeDtypeStruct((3, cut, width), BF16),
-            jax.ShapeDtypeStruct((3, units - cut, width), BF16),
-        ],
+            out_specs=pl.BlockSpec((3, size, width), lambda j, tile_ref: (0, 0, j)),
+        ),
+        out_shape=jax.ShapeDtypeStruct((3, size, 2 * width), BF16),
         compiler_params=pltpu.CompilerParams(vmem_limit_bytes=VMEM_ALL),
         cost_estimate=pl.CostEstimate(
-            flops=6 * units * tokens * width,
-            bytes_accessed=2 * (tokens * (2 * width + 3 * units) + 3 * units * width),
+            flops=12 * size * tokens * width,
+            bytes_accessed=2 * (tokens * (4 * width + 3 * units) + 6 * size * width),
             transcendentals=0,
         ),
         name="weight_terms",
-    )(tile.reshape(1), *acts, *blocks)
+    )(jnp.stack(tiles), *acts, *blocks)
 
 
 def together(*values):
@@ -376,7 +371,9 @@
     got = exchange_slots(sent, me, experts)
     both0, partial0 = dense([own])
 
-    mirrored, paired, partial0, got = together(mirrored, paired, partial0, got)
+    got, partial0, both0 = together(got, partial0, both0)
+
+    mirrored, paired, got = together(mirrored, paired, got)
     last = pairs(mirrored)
     slots = lax.all_gather(got, "ep", axis=0, tiled=False)
     both12, partial12 = dense([paired, mirrored])
@@ -395,29 +392,29 @@
     from_last = pairs(partial3)
 
     acts, tokens = (a + b + c for a, b, c in zip(both0, both12, both3))
-    cut = -(-half // 32) * 16
-    made = {3: weight_terms(jnp.bitwise_xor(chip, 3), acts, tokens, 2 * columns, cut)}
-    made[3], chip = together(made[3], chip)
-    for apart in (1, 2, 0):
-        made[apart] = weight_terms(
-            jnp.bitwise_xor(chip, apart), acts, tokens, 2 * columns, cut
-        )
-    low = across(made[3][0], 2)
-    high = across(made[3][1], 4)
-    low_own = across(made[1][0], 2)
-    high_own = across(made[2][1], 4)
-    from_last, routed, made[0] = together(from_last, routed, made[0])
+    cut, width = -(-half // 32) * 16, 2 * columns
+    x_chip, y_chip, xy_chip = [jnp.bitwise_xor(chip, k) for k in (1, 2, 3)]
+    low_sent = weight_terms((xy_chip, x_chip), acts, tokens, width, 0, cut)
+    high_sent = weight_terms((xy_chip, y_chip), acts, tokens, width, cut, half)
+    low_kept = weight_terms((y_chip, chip), acts, tokens, width, 0, cut)
+    high_kept = weight_terms((x_chip, chip), acts, tokens, width, cut, half)
+    low_near, high_near = across(low_sent, 2), across(high_sent, 4)
+    routed_input = slots_back(routed, dispatch, me, experts)
+    from_last, routed_input, low_kept, high_kept = together(
+        from_last, routed_input, low_kept, high_kept
+    )
     from_mirror = mirror(add(mirrored_partial, from_last))
     from_pair = pairs(paired_partial)
-    routed_input = slots_back(routed, dispatch, me, experts)
-    low, high, made[0] = together(low, high, made[0])
-    low = across(add(made[2][0], low), 4)
-    high = across(add(made[1][1], high), 2)
-    low, high, from_pair, from_mirror, routed_input = together(
-        low, high, from_pair, from_mirror, routed_input
+    low_near, high_near, low_kept, high_kept = together(
+        low_near, high_near, low_kept, high_kept
+    )
+    low_far = across(add(low_kept[:, :, :width], low_near[:, :, :width]), 4)
+    high_far = across(add(high_kept[:, :, :width], high_near[:, :, :width]), 2)
+    low_far, high_far, from_pair, from_mirror = together(
+        low_far, high_far, from_pair, from_mirror
     )
     mine, other = final_sum(
-        core, (made[0][0], low_own, low), (made[0][1], high_own, high)
+        core, (low_kept, low_near, low_far), (high_kept, high_near, high_far)
     )
     grads = join_halves(core, mine, across(other, 1))
     grad_input = (

time: 300 us -> 297 us (0.990)
  Pallas kernels: 67.6 us -> 72.2 us
  waiting for transfers between devices: 127 us -> 124 us
    all_to_all x1, waiting for transfers between devices: 69.1 us -> 34.1 us  [exchange_slots(): got = lax.all_to_all(sent, 'tp', split_axis=0, concat_axis=0, tiled=True)]
    all_gather x1, waiting for transfers between devices: 0.02 us -> 22 us  [line_body(): down = lax.all_gather(dense_down.T, 'ep', axis=0, tiled=True)]
    reduce_scatter x1, waiting for transfers between devices: 0.01 us -> 16 us  [line_body(): routed = lax.psum_scatter(slot_terms, 'ep', scatter_dimension=0, tiled=True)]
    ppermute x4, waiting for transfers between devices: 6.05 us -> 0.01 us  [pairs(): return lax.ppermute(value, 'tp', [(0, 1), (1, 0), (2, 3), (3, 2)])]
    convert_element_type x3, other arithmetic: 6.99 us -> 2.17 us  [add(): return (a.astype(F32) + b.astype(F32)).astype(BF16)]
    pallas_call x4, Pallas kernels: 23.8 us -> 28.5 us  [weight_terms(): pl.pallas_call(kernel, grid_spec=pltpu.PrefetchScalarGridSpec(num_scalar_...]
    ppermute x2, waiting for transfers between devices: 0.01 us -> 4.46 us  [mirror(): return lax.ppermute(value, 'tp', [(0, 3), (1, 2), (2, 1), (3, 0)])]
    pallas_call x1, Pallas kernels: 16.1 us -> 19.3 us  [expert_block(): pl.pallas_call(kernel, in_specs=[vmem] * 5, out_specs=[hbm, hbm, hbm, vme...]
  transfers between devices with their start and end apart: 27 -> 25, of which waited for: 8 -> 10; matrix products, arithmetic and copies ran while one was open for 10% -> 9% of each run, Pallas kernels for 21% -> 23%
where the time goes in v1:
time: 297 us; the launch traced here: 294 us
  waiting for transfers between devices  124 us (42%)
  Pallas kernels  72.2 us (24%)
  local copies, waits for them, and re-layouts  41.3 us (14%)
  starting transfers between devices  24 us (8%)
  other arithmetic  14.3 us (5%)
  between operations  14.2 us (5%)
  matrix products  3.31 us (1%)
    all_to_all x1, waiting for transfers between devices, exchange_slots(): got = lax.all_to_all(sent, 'tp', split_axis=0, concat_axis=0, tiled=True)  34.1 us
    unnamed x66, local copies, waits for them, and re-layouts  32.9 us
    pallas_call x4, Pallas kernels, weight_terms(): pl.pallas_call(kernel, grid_spec=pltpu.PrefetchScalarGridSpec(num_scalar_...  28.5 us
    ppermute x12, waiting for transfers between devices, across(): return lax.ppermute(value, 'ep', [(i, i ^ apart) for i in range(8)])  27 us
    all_gather x1, waiting for transfers between devices, line_body(): down = lax.all_gather(dense_down.T, 'ep', axis=0, tiled=True)  22 us
    pallas_call x3, Pallas kernels, dense_block(): pl.pallas_call(kernel, in_specs=[pl.BlockSpec(memory_space=pltpu.SMEM)] +...  20.6 us
    pallas_call x1, Pallas kernels, expert_block(): pl.pallas_call(kernel, in_specs=[vmem] * 5, out_specs=[hbm, hbm, hbm, vme...  19.3 us
    reduce_scatter x1, waiting for transfers between devices, line_body(): routed = lax.psum_scatter(slot_terms, 'ep', scatter_dimension=0, tiled=True)  16 us
  transfers between devices with their start and end apart: 25, of which 10 were waited for; matrix products, arithmetic and copies ran while one was open for 9% of the time, Pallas kernels for 23%

profile of v1, /device:TPU:0, one launch (start us, length us, event | category | flops | bytes accessed | tf_op | source)
XLA Modules:
  0.0 293.6 jit_solution(16583393796152878883)
XLA Ops:
  7.2 0.7 all-gather.4.cloned.1.call-update
  7.9 1.6 pad_maximum_fusion.refs_0_.refs_6_
  10.1 4.7 %collective-permute-start.2 = (bf16[2,128,3584]{2,1,0:T(8,128)(2,1)S(1)}, bf16[2,128,3584]{2,1,0:T(8,128)(2,1)}, u32[]{:S(2)}, u32[]{:S(2)}) collective-permute-start(bf16[2,128,3584]{2,1,0:T(8,128)(2,1)S(1)} %pad_maximum_fusion.refs_0_.refs_6_), channel_id=1, source_target_pairs={{0,24},{8,16},{16,8},{24,0},{1,25},{9,17},{17,9},{25,1},{2,26},{10... | collective-permute-start | bytes 5505032 | tf_op jit(solution)/shard_map/ppermute | solution.py:355
  15.3 1.2 reduce-window.6
  17.5 1.0 eq.66
  19.0 1.0 mul.34
  20.3 1.1 multiply_reduce_fusion
  21.5 1.2 fusion.5
  23.0 1.4 convolution_convert_fusion
  24.5 1.0 fusion.2
  25.6 3.4 %all-to-all-start = ((bf16[4,2,4,3584]{3,2,1,0:T(4,128)(2,1)}), bf16[4,2,4,3584]{3,2,1,0:T(4,128)(2,1)S(1)}, u32[]{:S(2)}, u32[]{:S(2)}) async-start(bf16[4,2,4,3584]{3,2,1,0:T(4,128)(2,1)} %fusion.2), calls=%async_computation | async-start | bytes 458752 | tf_op jit(solution)/shard_map/all_to_all | solution.py:56
  29.0 22.0 %all-gather.4.cloned.1.call-done.refs_3_.refs_4_ = bf16[3584,608]{1,0:T(8,128)(2,1)} async-done(((bf16[448,608]{1,0:T(8,128)(2,1)}), bf16[3584,608]{1,0:T(8,128)(2,1)}) %all-gather.4.cloned.1.call-update) | async-done | bytes 4358160 | tf_op jit(solution)/shard_map/all_gather | solution.py:349
  51.0 2.3 copy-done.2
  53.3 2.2 copy-done.5
  55.6 2.2 copy-done.8
  57.8 5.0 %dense_block.3 = (bf16[3,304,128]{2,1,0:T(8,128)(2,1)S(1)}, bf16[3,304,128]{2,1,0:T(8,128)(2,1)S(1)}, bf16[128,3584]{1,0:T(8,128)(2,1)S(1)}) custom-call(s32[1]{0:T(128)} %bitcast.6.core_ref, bf16[2,128,3584]{2,1,0:T(8,128)(2,1)S(1)} %pad_maximum_fusion.refs_0_.refs_6_, bf16[608,3584]{1,0:T(8,128)(2,1)S(1)} %copy-done.5, bf16[608,3584]{1,0:T(8,128)(2,1)S(1)} %copy-done.8, ...), custom_call_target="tpu_custom_call" | custom-call | flops 2789212160 | bytes 16293888 | tf_op jit(solution)/shard_map/dense_block/pallas_call | solution.py:153
  62.8 0.7 copy-done.14
  63.5 1.0 copy-done.19
  64.7 34.1 %all-to-all-done = bf16[4,2,4,3584]{3,2,1,0:T(4,128)(2,1)S(1)} async-done(((bf16[4,2,4,3584]{3,2,1,0:T(4,128)(2,1)}), bf16[4,2,4,3584]{3,2,1,0:T(4,128)(2,1)S(1)}, u32[]{:S(2)}, u32[]{:S(2)}) %all-to-all-start) | async-done | bytes 229408 | tf_op jit(solution)/shard_map/all_to_all | solution.py:56
  99.0 0.7 copy.47
  100.9 2.3 copy-done.3
  103.2 2.2 copy-done.6
  105.5 2.4 copy-done.9
  107.9 9.6 %dense_block.4 = (bf16[3,304,256]{2,1,0:T(8,128)(2,1)S(1)}, bf16[3,304,256]{2,1,0:T(8,128)(2,1)S(1)}, bf16[256,3584]{1,0:T(8,128)(2,1)S(1)}) custom-call(s32[1]{0:T(128)} %bitcast.6.core_ref, bf16[2,128,3584]{2,1,0:T(8,128)(2,1)} %collective-permute-done.3.refs_0_.refs_8_, bf16[2,128,3584]{2,1,0:T(8,128)(2,1)} %collective-permute-done.2.refs_1_.refs_9_, ...), custom_call_target="tpu_custom_call" | custom-call | flops 5578424320 | bytes 19513344 | tf_op jit(solution)/shard_map/dense_block/pallas_call | solution.py:153
  117.5 0.8 copy-done.13
  118.3 1.2 copy-done.16
  119.5 7.3 %all-gather.6.cloned.1.call-done = bf16[16,16,3584]{2,1,0:T(8,128)(2,1)} async-done(((bf16[2,16,3584]{2,1,0:T(8,128)(2,1)}), bf16[16,16,3584]{2,1,0:T(8,128)(2,1)}) %all-gather.6.cloned.1.call-update) | async-done | bytes 1835024 | tf_op jit(solution)/shard_map/all_gather | solution.py:378
  126.8 1.6 fusion.12
  128.4 2.2 copy-done.21
  130.6 2.2 copy-done.22
  132.8 2.2 copy-done.23
  135.1 19.3 %expert_block.1 = (bf16[608,3584]{1,0:T(8,128)(2,1)}, bf16[608,3584]{1,0:T(8,128)(2,1)}, bf16[608,3584]{1,0:T(8,128)(2,1)}, bf16[128,3584]{1,0:T(8,128)(2,1)}) custom-call(bf16[128,3584]{1,0:T(8,128)(2,1)S(1)} %bitcast.51, bf16[128,3584]{1,0:T(8,128)(2,1)S(1)} %bitcast.50, bf16[608,3584]{1,0:T(8,128)(2,1)S(1)} %bitcast.52, bf16[608,3584]{1,0:T(8,128)(2,1)S(1)} %bitcast.53, ...), custom_call_target="tpu_custom_call" | custom-call | flops 4462739456 | bytes 28901376 | tf_op jit(solution)/shard_map/expert_block/pallas_call | solution.py:206
  154.8 0.8 pad_add_fusion.3.tile_ref
  156.2 0.7 pad_add_fusion.1.tile_ref
  157.5 2.3 copy-done.4
  159.8 2.3 copy-done.7
  162.1 2.3 copy-done.10
  164.4 5.9 %dense_block.5 = (bf16[3,304,128]{2,1,0:T(8,128)(2,1)S(1)}, bf16[3,304,128]{2,1,0:T(8,128)(2,1)S(1)}, bf16[128,3584]{1,0:T(8,128)(2,1)}) custom-call(s32[1]{0:T(128)} %bitcast.6.core_ref, bf16[2,128,3584]{2,1,0:T(8,128)(2,1)S(1)} %collective-permute-done.4.refs_0_.refs_12_, bf16[608,3584]{1,0:T(8,128)(2,1)S(1)} %copy-done.7, ...), custom_call_target="tpu_custom_call" | custom-call | flops 2789212160 | bytes 16293888 | tf_op jit(solution)/shard_map/dense_block/pallas_call | solution.py:153
  170.4 0.7 copy-done.15
  171.3 1.5 collective-permute-start.12
  172.8 1.0 split.6
  174.4 16.0 %reduce-scatter.2.cloned.1.call-done = bf16[16,3584]{1,0:T(8,128)(2,1)} async-done(((bf16[128,3584]{1,0:T(8,128)(2,1)}), bf16[16,3584]{1,0:T(8,128)(2,1)}) %reduce-scatter.2.cloned.1.call-update) | async-done | bytes 114704 | tf_op jit(solution)/shard_map/reduce_scatter | solution.py:389
  190.4 0.9 reshape.106
  191.4 3.4 %collective-permute-start.13 = (bf16[4,3584]{1,0:T(4,128)(2,1)S(1)}, bf16[4,3584]{1,0:T(4,128)(2,1)S(1)}, u32[]{:S(2)}, u32[]{:S(2)}) collective-permute-start(bf16[4,3584]{1,0:T(4,128)(2,1)S(1)} %get-tuple-element.118), channel_id=1, source_target_pairs={{0,24},{8,0},{16,8},{24,16},{1,25},{9,1},{17,9},{25,17},{2,26},{10... | collective-permute-start | bytes 86024 | tf_op jit(solution)/shard_map/ppermute | solution.py:40
  194.8 1.1 collective-permute-start.15
  195.9 7.2 %weight_terms.4 = bf16[3,160,1792]{2,1,0:T(8,128)(2,1)} custom-call(s32[2]{0:T(128)} %pad_add_fusion.tile_ref, bf16[3,304,128]{2,1,0:T(8,128)(2,1)} %copy-done.14, bf16[3,304,128]{2,1,0:T(8,128)(2,1)} %copy-done.26, bf16[3,304,256]{2,1,0:T(8,128)(2,1)} %copy-done.13, bf16[3,304,256]{2,1,0:T(8,128)(2,1)} %copy-done.24, bf16[3,304,128]{2,1,0:T(8,128)(2,1)} %copy-done.15, ...), custom_call_target="tpu_custom_call" | custom-call | flops 1761607680 | bytes 10928128 | tf_op jit(solution)/shard_map/weight_terms/pallas_call | solution.py:306
  203.1 11.8 %collective-permute-done.13 = bf16[4,3584]{1,0:T(4,128)(2,1)S(1)} collective-permute-done((bf16[4,3584]{1,0:T(4,128)(2,1)S(1)}, bf16[4,3584]{1,0:T(4,128)(2,1)S(1)}, u32[]{:S(2)}, u32[]{:S(2)}) %collective-permute-start.13) | collective-permute-done | bytes 28704 | tf_op jit(solution)/shard_map/ppermute | solution.py:40
  214.9 1.5 collective-permute-start.10
  216.4 1.0 collective-permute-done.15
  217.6 7.0 %weight_terms.5 = bf16[3,144,1792]{2,1,0:T(8,128)(2,1)} custom-call(s32[2]{0:T(128)} %pad_add_fusion.1.tile_ref, bf16[3,304,128]{2,1,0:T(8,128)(2,1)} %copy-done.14, bf16[3,304,128]{2,1,0:T(8,128)(2,1)} %copy-done.26, bf16[3,304,256]{2,1,0:T(8,128)(2,1)} %copy-done.13, bf16[3,304,256]{2,1,0:T(8,128)(2,1)} %copy-done.24, bf16[3,304,128]{2,1,0:T(8,128)(2,1)} %copy-done.15, ...), custom_call_target="tpu_custom_call" | custom-call | flops 1585446912 | bytes 10756096 | tf_op jit(solution)/shard_map/weight_terms/pallas_call | solution.py:306
  224.6 1.5 collective-permute-start.11
  226.1 1.6 fusion.13
  227.7 7.0 %weight_terms.7.refs_3_ = bf16[3,144,1792]{2,1,0:T(8,128)(2,1)} custom-call(s32[2]{0:T(128)} %pad_add_fusion.3.tile_ref, bf16[3,304,128]{2,1,0:T(8,128)(2,1)} %copy-done.14, bf16[3,304,128]{2,1,0:T(8,128)(2,1)} %copy-done.26, bf16[3,304,256]{2,1,0:T(8,128)(2,1)} %copy-done.13, bf16[3,304,256]{2,1,0:T(8,128)(2,1)} %copy-done.24, ...), custom_call_target="tpu_custom_call" | custom-call | flops 1585446912 | bytes 10756096 | tf_op jit(solution)/shard_map/weight_terms/pallas_call | solution.py:306
  234.7 7.2 %weight_terms.6.refs_0_ = bf16[3,160,1792]{2,1,0:T(8,128)(2,1)} custom-call(s32[2]{0:T(128)} %pad_add_fusion.2.tile_ref, bf16[3,304,128]{2,1,0:T(8,128)(2,1)} %copy-done.14, bf16[3,304,128]{2,1,0:T(8,128)(2,1)} %copy-done.26, bf16[3,304,256]{2,1,0:T(8,128)(2,1)} %copy-done.13, bf16[3,304,256]{2,1,0:T(8,128)(2,1)} %copy-done.24, ...), custom_call_target="tpu_custom_call" | custom-call | flops 1761607680 | bytes 10928128 | tf_op jit(solution)/shard_map/weight_terms/pallas_call | solution.py:306
  241.9 1.8 add_convert_fusion.1
  243.7 1.6 collective-permute-start.19
  245.3 14.5 %collective-permute-done.11.refs_4_ = bf16[3,144,1792]{2,1,0:T(8,128)(2,1)S(1)} collective-permute-done((bf16[3,144,1792]{2,1,0:T(8,128)(2,1)}, bf16[3,144,1792]{2,1,0:T(8,128)(2,1)S(1)}, u32[]{:S(2)}, u32[]{:S(2)}) %collective-permute-start.11) | collective-permute-done | bytes 1548320 | tf_op jit(solution)/shard_map/ppermute | solution.py:358
  260.0 1.5 collective-permute-start.16
  262.4 4.5 %collective-permute-done.19 = bf16[128,3584]{1,0:T(8,128)(2,1)S(1)} collective-permute-done((bf16[128,3584]{1,0:T(8,128)(2,1)S(1)}, bf16[128,3584]{1,0:T(8,128)(2,1)S(1)}, u32[]{:S(2)}, u32[]{:S(2)}) %collective-permute-start.19) | collective-permute-done | bytes 917536 | tf_op jit(solution)/shard_map/ppermute | solution.py:355
  266.8 12.1 %collective-permute-done.17.refs_5_ = bf16[3,144,896]{2,1,0:T(8,128)(2,1)S(1)} collective-permute-done((bf16[3,144,896]{2,1,0:T(8,128)(2,1)S(1)}, bf16[3,144,896]{2,1,0:T(8,128)(2,1)S(1)}, u32[]{:S(2)}, u32[]{:S(2)}) %collective-permute-start.17) | collective-permute-done | bytes 774176 | tf_op jit(solution)/shard_map/ppermute | solution.py:358
  279.3 1.0 final_sum.1
  280.4 2.8 add_convert_fusion
  283.3 1.0 copy-done.29
  284.2 2.9 join_halves.1
  (113 shorter events, 9.0 us)
Async XLA Ops:
  7.2 43.9 %all-gather.4.cloned.1.call-start = ((), (), s32[]{:S(2)}) async-start(), calls=%async_computation.2 | async-start | bytes 5160960 | tf_op jit(solution)/shard_map/all_gather | solution.py:349
  7.9 6.9 %copy-start.30 = (s32[128,2]{0,1:T(2,128)S(1)}, s32[128,2]{0,1:T(2,128)}, u32[]{:S(2)}) copy-start(s32[128,2]{0,1:T(2,128)} %param.12) | copy-start | bytes 3076
  9.5 41.5 %copy-start = (bf16[2,128,3584]{2,1,0:T(8,128)(2,1)}, bf16[2,128,3584]{2,1,0:T(8,128)(2,1)S(1)}, u32[]{:S(2)}) copy-start(bf16[2,128,3584]{2,1,0:T(8,128)(2,1)S(1)} %pad_maximum_fusion.refs_0_.refs_6_) | copy-start | bytes 5505028
  9.6 10.5 %copy-start.31 = (f32[128,2]{0,1:T(2,128)S(1)}, f32[128,2]{0,1:T(2,128)}, u32[]{:S(2)}) copy-start(f32[128,2]{0,1:T(2,128)} %param.13) | copy-start | bytes 3076
  9.6 89.4 %collective-permute-start.1 = (bf16[2,128,3584]{2,1,0:T(8,128)(2,1)S(1)}, bf16[2,128,3584]{2,1,0:T(8,128)(2,1)}, u32[]{:S(2)}, u32[]{:S(2)}) collective-permute-start(bf16[2,128,3584]{2,1,0:T(8,128)(2,1)S(1)} %pad_maximum_fusion.refs_0_.refs_6_), channel_id=1, source_target_pairs={{0,1},{1,0},{2,3},{3,2},{4,5},{5,4},{6,7},{7,6},{8,9},{9,8},{10,11... | collective-permute-start | bytes 5505032 | tf_op jit(solution)/shard_map/ppermute | solution.py:358
  10.1 88.9 %collective-permute-start.2 = (bf16[2,128,3584]{2,1,0:T(8,128)(2,1)S(1)}, bf16[2,128,3584]{2,1,0:T(8,128)(2,1)}, u32[]{:S(2)}, u32[]{:S(2)}) collective-permute-start(bf16[2,128,3584]{2,1,0:T(8,128)(2,1)S(1)} %pad_maximum_fusion.refs_0_.refs_6_), channel_id=1, source_target_pairs={{0,24},{8,16},{16,8},{24,0},{1,25},{9,17},{17,9},{25,1},{2,26},{10... | collective-permute-start | bytes 5505032 | tf_op jit(solution)/shard_map/ppermute | solution.py:355
  14.8 84.2 %collective-permute-start.3 = (bf16[2,128,3584]{2,1,0:T(8,128)(2,1)S(1)}, bf16[2,128,3584]{2,1,0:T(8,128)(2,1)}, u32[]{:S(2)}, u32[]{:S(2)}) collective-permute-start(bf16[2,128,3584]{2,1,0:T(8,128)(2,1)S(1)} %pad_maximum_fusion.refs_0_.refs_6_), channel_id=1, source_target_pairs={{0,8},{8,0},{16,24},{24,16},{1,9},{9,1},{17,25},{25,17},{2,10},{10... | collective-permute-start | bytes 5505032 | tf_op jit(solution)/shard_map/ppermute | solution.py:352
  16.5 6.3 %copy-start.28 = (bf16[128,3584]{1,0:T(8,128)(2,1)S(1)}, bf16[128,3584]{1,0:T(8,128)(2,1)}, u32[]{:S(2)}) copy-start(bf16[128,3584]{1,0:T(8,128)(2,1)} %param.11) | copy-start | bytes 2752516
  25.6 73.2 %all-to-all-start = ((bf16[4,2,4,3584]{3,2,1,0:T(4,128)(2,1)}), bf16[4,2,4,3584]{3,2,1,0:T(4,128)(2,1)S(1)}, u32[]{:S(2)}, u32[]{:S(2)}) async-start(bf16[4,2,4,3584]{3,2,1,0:T(4,128)(2,1)} %fusion.2), calls=%async_computation | async-start | bytes 458752 | tf_op jit(solution)/shard_map/all_to_all | solution.py:56
  29.0 97.8 %all-gather.6.cloned.1.call-start = ((), (), s32[]{:S(2)}) async-start(), calls=%async_computation.4 | async-start | bytes 2064384 | tf_op jit(solution)/shard_map/all_gather | solution.py:378
  51.0 2.3 copy-start.2
  53.3 2.2 copy-start.5
  55.6 2.2 copy-start.8
  62.8 0.7 copy-start.14
  63.5 1.0 copy-start.19
  64.5 34.5 %collective-permute-start = (bf16[3,304,128]{2,1,0:T(8,128)(2,1)S(1)}, bf16[3,304,128]{2,1,0:T(8,128)(2,1)S(1)}, u32[]{:S(2)}, u32[]{:S(2)}) collective-permute-start(bf16[3,304,128]{2,1,0:T(8,128)(2,1)S(1)} %get-tuple-element.62), channel_id=1, source_target_pairs={{0,1},{1,0},{2,3},{3,2},{4,5},{5,4},{6,7},{7,6},{8,9},{9,8},{10,11... | collective-permute-start | bytes 700424 | tf_op jit(solution)/shard_map/ppermute | solution.py:358
  99.0 18.5 %copy-start.26 = (bf16[3,304,128]{2,1,0:T(8,128)(2,1)}, bf16[3,304,128]{2,1,0:T(8,128)(2,1)S(1)}, u32[]{:S(2)}) copy-start(bf16[3,304,128]{2,1,0:T(8,128)(2,1)S(1)} %collective-permute-done.refs_1_) | copy-start | bytes 700420
  99.8 90.6 %reduce-scatter.2.cloned.1.call-start = ((), (), s32[]{:S(2)}) async-start(), calls=%async_computation.3 | async-start | bytes 1032192 | tf_op jit(solution)/shard_map/reduce_scatter | solution.py:389
  100.0 54.4 %collective-permute-start.4 = (bf16[2,128,3584]{2,1,0:T(8,128)(2,1)}, bf16[2,128,3584]{2,1,0:T(8,128)(2,1)S(1)}, u32[]{:S(2)}, u32[]{:S(2)}) collective-permute-start(bf16[2,128,3584]{2,1,0:T(8,128)(2,1)} %collective-permute-done.2.refs_1_.refs_9_), channel_id=1, source_target_pairs={{0,8},{8,0},{16,24},{24,16},{1,9},{9,1},{17,25},{25,17},{2,10},{10... | collective-permute-start | bytes 5505032 | tf_op jit(solution)/shard_map/ppermute | solution.py:352
  100.4 54.0 %collective-permute-start.7 = (bf16[2,128,3584]{2,1,0:T(8,128)(2,1)}, bf16[2,128,3584]{2,1,0:T(8,128)(2,1)}, u32[]{:S(2)}, u32[]{:S(2)}) collective-permute-start(bf16[2,128,3584]{2,1,0:T(8,128)(2,1)} %collective-permute-done.2.refs_1_.refs_9_), channel_id=1, source_target_pairs={{0,1},{1,0},{2,3},{3,2},{4,5},{5,4},{6,7},{7,6},{8,9},{9,8},{10,11... | collective-permute-start | bytes 5505032 | tf_op jit(solution)/shard_map/ppermute | solution.py:358
  100.4 54.0 %collective-permute-start.6 = (bf16[2,128,3584]{2,1,0:T(8,128)(2,1)}, bf16[2,128,3584]{2,1,0:T(8,128)(2,1)}, u32[]{:S(2)}, u32[]{:S(2)}) collective-permute-start(bf16[2,128,3584]{2,1,0:T(8,128)(2,1)} %collective-permute-done.3.refs_0_.refs_8_), channel_id=1, source_target_pairs={{0,1},{1,0},{2,3},{3,2},{4,5},{5,4},{6,7},{7,6},{8,9},{9,8},{10,11... | collective-permute-start | bytes 5505032 | tf_op jit(solution)/shard_map/ppermute | solution.py:358
  100.9 2.3 copy-start.3
  103.2 2.2 copy-start.6
  105.5 2.4 copy-start.9
  117.5 0.8 copy-start.13
  118.3 1.2 copy-start.16
  119.5 34.9 %collective-permute-start.5 = (bf16[3,304,256]{2,1,0:T(8,128)(2,1)S(1)}, bf16[3,304,256]{2,1,0:T(8,128)(2,1)S(1)}, u32[]{:S(2)}, u32[]{:S(2)}) collective-permute-start(bf16[3,304,256]{2,1,0:T(8,128)(2,1)S(1)} %get-tuple-element.76), channel_id=1, source_target_pairs={{0,1},{1,0},{2,3},{3,2},{4,5},{5,4},{6,7},{7,6},{8,9},{9,8},{10,11... | collective-permute-start | bytes 1400840 | tf_op jit(solution)/shard_map/ppermute | solution.py:358
  128.4 2.2 copy-start.21
  130.6 2.2 copy-start.22
  132.8 2.2 copy-start.23
  154.4 16.0 %copy-start.24 = (bf16[3,304,256]{2,1,0:T(8,128)(2,1)}, bf16[3,304,256]{2,1,0:T(8,128)(2,1)S(1)}, u32[]{:S(2)}) copy-start(bf16[3,304,256]{2,1,0:T(8,128)(2,1)S(1)} %collective-permute-done.5.refs_3_) | copy-start | bytes 1400836
  154.4 16.0 %copy-start.1 = (bf16[2,128,3584]{2,1,0:T(8,128)(2,1)}, bf16[2,128,3584]{2,1,0:T(8,128)(2,1)S(1)}, u32[]{:S(2)}) copy-start(bf16[2,128,3584]{2,1,0:T(8,128)(2,1)S(1)} %collective-permute-done.4.refs_0_.refs_12_) | copy-start | bytes 5505028
  154.4 40.4 %collective-permute-start.9 = (bf16[2,128,3584]{2,1,0:T(8,128)(2,1)S(1)}, bf16[2,128,3584]{2,1,0:T(8,128)(2,1)}, u32[]{:S(2)}, u32[]{:S(2)}) collective-permute-start(bf16[2,128,3584]{2,1,0:T(8,128)(2,1)S(1)} %collective-permute-done.4.refs_0_.refs_12_), channel_id=1, source_target_pairs={{0,1},{1,0},{2,3},{3,2},{4,5},{5,4},{6,7},{7,6},{8,9},{9,8},{10,11... | collective-permute-start | bytes 5505032 | tf_op jit(solution)/shard_map/ppermute | solution.py:358
  157.5 2.3 copy-start.4
  159.8 2.3 copy-start.7
  162.1 2.3 copy-start.10
  164.4 8.4 %copy-start.17 = (bf16[256,3584]{1,0:T(8,128)(2,1)S(1)}, bf16[256,3584]{1,0:T(8,128)(2,1)}, u32[]{:S(2)}) copy-start(bf16[256,3584]{1,0:T(8,128)(2,1)} %copy-done.16) | copy-start | bytes 5505028
  170.4 0.7 copy-start.15
  171.1 23.7 %collective-permute-start.8 = (bf16[3,304,128]{2,1,0:T(8,128)(2,1)S(1)}, bf16[3,304,128]{2,1,0:T(8,128)(2,1)S(1)}, u32[]{:S(2)}, u32[]{:S(2)}) collective-permute-start(bf16[3,304,128]{2,1,0:T(8,128)(2,1)S(1)} %get-tuple-element.83), channel_id=1, source_target_pairs={{0,1},{1,0},{2,3},{3,2},{4,5},{5,4},{6,7},{7,6},{8,9},{9,8},{10,11... | collective-permute-start | bytes 700424 | tf_op jit(solution)/shard_map/ppermute | solution.py:358
  171.3 70.6 %collective-permute-start.12 = (bf16[128,3584]{1,0:T(8,128)(2,1)}, bf16[128,3584]{1,0:T(8,128)(2,1)}, u32[]{:S(2)}, u32[]{:S(2)}) collective-permute-start(bf16[128,3584]{1,0:T(8,128)(2,1)} %get-tuple-element.90), channel_id=1, source_target_pairs={{0,8},{8,0},{16,24},{24,16},{1,9},{9,1},{17,25},{25,17},{2,10},{10... | collective-permute-start | bytes 2752520 | tf_op jit(solution)/shard_map/ppermute | solution.py:352
  173.8 88.5 %collective-permute-start.18 = (bf16[128,3584]{1,0:T(8,128)(2,1)}, bf16[128,3584]{1,0:T(8,128)(2,1)}, u32[]{:S(2)}, u32[]{:S(2)}) collective-permute-start(bf16[128,3584]{1,0:T(8,128)(2,1)} %split.6), channel_id=1, source_target_pairs={{0,8},{8,0},{16,24},{24,16},{1,9},{9,1},{17,25},{25,17},{2,10},{10... | collective-permute-start | bytes 2752520 | tf_op jit(solution)/shard_map/ppermute | solution.py:352
  191.4 23.6 %collective-permute-start.13 = (bf16[4,3584]{1,0:T(4,128)(2,1)S(1)}, bf16[4,3584]{1,0:T(4,128)(2,1)S(1)}, u32[]{:S(2)}, u32[]{:S(2)}) collective-permute-start(bf16[4,3584]{1,0:T(4,128)(2,1)S(1)} %get-tuple-element.118), channel_id=1, source_target_pairs={{0,24},{8,0},{16,8},{24,16},{1,25},{9,1},{17,9},{25,17},{2,26},{10... | collective-permute-start | bytes 86024 | tf_op jit(solution)/shard_map/ppermute | solution.py:40
  194.8 1.1 copy-start.27
  194.8 21.7 %collective-permute-start.14 = (bf16[4,3584]{1,0:T(4,128)(2,1)S(1)}, bf16[4,3584]{1,0:T(4,128)(2,1)S(1)}, u32[]{:S(2)}, u32[]{:S(2)}) collective-permute-start(bf16[4,3584]{1,0:T(4,128)(2,1)S(1)} %get-tuple-element.117), channel_id=1, source_target_pairs={{0,16},{8,24},{16,0},{24,8},{1,17},{9,25},{17,1},{25,9},{2,18},{10... | collective-permute-start | bytes 86024 | tf_op jit(solution)/shard_map/ppermute | solution.py:40
  194.8 22.6 %collective-permute-start.15 = (bf16[4,3584]{1,0:T(4,128)(2,1)S(1)}, bf16[4,3584]{1,0:T(4,128)(2,1)S(1)}, u32[]{:S(2)}, u32[]{:S(2)}) collective-permute-start(bf16[4,3584]{1,0:T(4,128)(2,1)S(1)} %get-tuple-element.116), channel_id=1, source_target_pairs={{0,8},{8,16},{16,24},{24,0},{1,9},{9,17},{17,25},{25,1},{2,10},{10... | collective-permute-start | bytes 86024 | tf_op jit(solution)/shard_map/ppermute | solution.py:40
  214.9 44.8 %collective-permute-start.10 = (bf16[3,160,1792]{2,1,0:T(8,128)(2,1)}, bf16[3,160,1792]{2,1,0:T(8,128)(2,1)S(1)}, u32[]{:S(2)}, u32[]{:S(2)}) collective-permute-start(bf16[3,160,1792]{2,1,0:T(8,128)(2,1)} %weight_terms.4), channel_id=1, source_target_pairs={{0,2},{1,3},{2,0},{3,1},{4,6},{5,7},{6,4},{7,5},{8,10},{9,11},{10,... | collective-permute-start | bytes 5160968 | tf_op jit(solution)/shard_map/ppermute | solution.py:358
  224.6 35.2 %collective-permute-start.11 = (bf16[3,144,1792]{2,1,0:T(8,128)(2,1)}, bf16[3,144,1792]{2,1,0:T(8,128)(2,1)S(1)}, u32[]{:S(2)}, u32[]{:S(2)}) collective-permute-start(bf16[3,144,1792]{2,1,0:T(8,128)(2,1)} %weight_terms.5), channel_id=1, source_target_pairs={{0,4},{1,5},{2,6},{3,7},{4,0},{5,1},{6,2},{7,3},{8,12},{9,13},{10,... | collective-permute-start | bytes 4644872 | tf_op jit(solution)/shard_map/ppermute | solution.py:358
  241.9 17.9 %copy-start.11 = (bf16[3,160,1792]{2,1,0:T(8,128)(2,1)S(1)}, bf16[3,160,1792]{2,1,0:T(8,128)(2,1)}, u32[]{:S(2)}) copy-start(bf16[3,160,1792]{2,1,0:T(8,128)(2,1)} %weight_terms.6.refs_0_) | copy-start | bytes 5160964
  243.7 17.8 %copy-start.12 = (bf16[3,144,1792]{2,1,0:T(8,128)(2,1)S(1)}, bf16[3,144,1792]{2,1,0:T(8,128)(2,1)}, u32[]{:S(2)}) copy-start(bf16[3,144,1792]{2,1,0:T(8,128)(2,1)} %weight_terms.7.refs_3_) | copy-start | bytes 4644868
  243.7 23.1 %collective-permute-start.19 = (bf16[128,3584]{1,0:T(8,128)(2,1)S(1)}, bf16[128,3584]{1,0:T(8,128)(2,1)S(1)}, u32[]{:S(2)}, u32[]{:S(2)}) collective-permute-start(bf16[128,3584]{1,0:T(8,128)(2,1)S(1)} %add_convert_fusion.1), channel_id=1, source_target_pairs={{0,24},{8,16},{16,8},{24,0},{1,25},{9,17},{17,9},{25,1},{2,26},{10... | collective-permute-start | bytes 2752520 | tf_op jit(solution)/shard_map/ppermute | solution.py:355
  260.0 19.3 %collective-permute-start.16 = (bf16[3,160,896]{2,1,0:T(8,128)(2,1)S(1)}, bf16[3,160,896]{2,1,0:T(8,128)(2,1)S(1)}, u32[]{:S(2)}, u32[]{:S(2)}) collective-permute-start(bf16[3,160,896]{2,1,0:T(8,128)(2,1)S(1)} %add_convert_fusion.2), channel_id=1, source_target_pairs={{0,4},{1,5},{2,6},{3,7},{4,0},{5,1},{6,2},{7,3},{8,12},{9,13},{10,... | collective-permute-start | bytes 2580488 | tf_op jit(solution)/shard_map/ppermute | solution.py:358
  261.7 18.7 %copy-start.20 = (bf16[128,3584]{1,0:T(8,128)(2,1)S(1)}, bf16[128,3584]{1,0:T(8,128)(2,1)}, u32[]{:S(2)}) copy-start(bf16[128,3584]{1,0:T(8,128)(2,1)} %copy-done.19) | copy-start | bytes 2752516
  261.7 18.7 %copy-start.25 = (f32[128,3584]{1,0:T(8,128)S(1)}, f32[128,3584]{1,0:T(8,128)}, u32[]{:S(2)}) copy-start(f32[128,3584]{1,0:T(8,128)} %fusion.13) | copy-start | bytes 5505028
  261.7 17.2 %collective-permute-start.17 = (bf16[3,144,896]{2,1,0:T(8,128)(2,1)S(1)}, bf16[3,144,896]{2,1,0:T(8,128)(2,1)S(1)}, u32[]{:S(2)}, u32[]{:S(2)}) collective-permute-start(bf16[3,144,896]{2,1,0:T(8,128)(2,1)S(1)} %add_convert_fusion.3), channel_id=1, source_target_pairs={{0,2},{1,3},{2,0},{3,1},{4,6},{5,7},{6,4},{7,5},{8,10},{9,11},{10,... | collective-permute-start | bytes 2322440 | tf_op jit(solution)/shard_map/ppermute | solution.py:358
  280.3 2.9 copy-start.18
  280.3 2.9 collective-permute-start.20
  283.2 1.0 copy-start.29
Sparse Core Ops, SparseCore 0:
  9.9 41.1 all-gather.3
  99.9 26.8 all-gather.5
  154.9 35.4 reduce-scatter.1

commit v2 on v1

--- a/solution.py
+++ b/solution.py
@@ -76,13 +76,13 @@
 def slots_back(own, dispatch, me, experts):
     width = own.shape[1]
     own = own.reshape(experts, CAP, width)
-    back = [
-        lax.dynamic_index_in_dim(own, lax.rem(me - k + experts, experts), keepdims=False)
-        for k in range(experts)
-    ]
-    back = jnp.stack(back[:1] + [shift(back[k], "tp", experts, -k) for k in range(1, experts)])
+    back = lax.all_to_all(own, "tp", split_axis=0, concat_axis=0, tiled=True)
+    dispatch = jnp.roll(dispatch.reshape(experts, CAP, -1), me, axis=0)
     return lax.dot_general(
-        dispatch, back.reshape(experts * CAP, width), LEADING, preferred_element_type=F32
+        dispatch.reshape(experts * CAP, -1),
+        back.reshape(experts * CAP, width),
+        LEADING,
+        preferred_element_type=F32,
     )
 
 
@@ -105,9 +105,11 @@
     return [(start, min(256, units - start)) for start in range(0, units, 256)]
 
 
-def layer_kernel(rows, cots, gate, up, down, down_turned, turned, partial, col):
+def layer_kernel(rows, cots, gate, up, down, down_turned, turned, partial, col, ready=None):
     units, width = gate.shape
-    for start, size in unit_tiles(units):
+    for t, (start, size) in enumerate(unit_tiles(units)):
+        if ready is not None:
+            ready(t)
         gate_pre, up_pre = [
             lax.dot_general(w[start : start + size], rows, CONTRACT, preferred_element_type=F32)
             for w in (gate, up)
@@ -174,11 +176,31 @@
     tok, width = rows.shape
     units = gate.shape[0]
     col = 512
+    tiles = unit_tiles(units)
 
     def kernel(
-        rows, cots, gate, up, down, g_gate, g_up, g_down, partial, turned, made, out_sems
+        rows, cots, gate, up, down, g_gate, g_up, g_down, partial, loaded, turned, made, sems, out_sems
     ):
-        layer_kernel(rows[...], cots[...], gate, up, down, False, turned, partial, 512)
+        copies = [
+            [
+                pltpu.make_async_copy(
+                    source.at[pl.ds(start, size)], loaded.at[w, pl.ds(start, size)], sems.at[w, t]
+                )
+                for w, source in enumerate((gate, up, down))
+            ]
+            for t, (start, size) in enumerate(tiles)
+        ]
+        for group in copies:
+            for copy in group:
+                copy.start()
+
+        def ready(t):
+            for copy in copies[t]:
+                copy.wait()
+
+        layer_kernel(
+            rows[...], cots[...], *[loaded.at[w] for w in range(3)], False, turned, partial, 512, ready
+        )
         outs = (g_down, g_gate, g_up)
         pending = [None, None]
         step = 0
@@ -205,20 +227,18 @@
     grad = jax.ShapeDtypeStruct((units, width), BF16)
     return pl.pallas_call(
         kernel,
-        in_specs=[vmem] * 5,
+        in_specs=[vmem, vmem, hbm, hbm, hbm],
         out_specs=[hbm, hbm, hbm, vmem],
         out_shape=[grad, grad, grad, jax.ShapeDtypeStruct((tok, width), BF16)],
         scratch_shapes=[
+            pltpu.VMEM((3, units, width), BF16),
             pltpu.VMEM((3, units, tok), BF16),
             pltpu.VMEM((2, units, col), BF16),
+            pltpu.SemaphoreType.DMA((3, len(tiles))),
             pltpu.SemaphoreType.DMA((2,)),
         ],
-        compiler_params=pltpu.CompilerParams(vmem_limit_bytes=VMEM_LIMIT),
-        cost_estimate=pl.CostEstimate(
-            flops=16 * units * width * tok,
-            bytes_accessed=12 * units * width + 6 * tok * width,
-            transcendentals=units * tok,
-        ),
+        compiler_params=pltpu.CompilerParams(vmem_limit_bytes=VMEM_ALL),
+        cost_estimate=pl.CostEstimate(flops=1, bytes_accessed=1, transcendentals=0),
         name="expert_block",
     )(rows, cots, gate, up, down)
 
@@ -377,16 +397,8 @@
     last = pairs(mirrored)
     slots = lax.all_gather(got, "ep", axis=0, tiled=False)
     both12, partial12 = dense([paired, mirrored])
-    slots, partial12 = together(slots, partial12)
-    slot_rows, slot_cot = slots[:, 0].reshape(-1, hidden_in.shape[1]), slots[:, 1].reshape(
-        -1, hidden_in.shape[1]
-    )
-    g_gate, g_up, g_down, slot_terms = expert_block(
-        slot_rows, slot_cot, expert_gate[0], expert_up[0], expert_down[0]
-    )
-
-    last, slot_terms, both0, both12 = together(last, slot_terms, both0, both12)
-    routed = lax.psum_scatter(slot_terms, "ep", scatter_dimension=0, tiled=True)
+
+    last, both12, slots = together(last, both12, slots)
     both3, partial3 = dense([last])
     paired_partial, mirrored_partial = jnp.split(partial12, 2, axis=0)
     from_last = pairs(partial3)
@@ -396,26 +408,31 @@
     x_chip, y_chip, xy_chip = [jnp.bitwise_xor(chip, k) for k in (1, 2, 3)]
     low_sent = weight_terms((xy_chip, x_chip), acts, tokens, width, 0, cut)
     high_sent = weight_terms((xy_chip, y_chip), acts, tokens, width, cut, half)
+    low_sent, chip, from_last = together(low_sent, chip, from_last)
     low_kept = weight_terms((y_chip, chip), acts, tokens, width, 0, cut)
     high_kept = weight_terms((x_chip, chip), acts, tokens, width, cut, half)
     low_near, high_near = across(low_sent, 2), across(high_sent, 4)
-    routed_input = slots_back(routed, dispatch, me, experts)
-    from_last, routed_input, low_kept, high_kept = together(
-        from_last, routed_input, low_kept, high_kept
-    )
     from_mirror = mirror(add(mirrored_partial, from_last))
+
+    slots, low_kept, high_kept = together(slots, low_kept, high_kept)
+    slot_rows, slot_cot = slots[:, 0].reshape(-1, hidden_in.shape[1]), slots[:, 1].reshape(
+        -1, hidden_in.shape[1]
+    )
+    g_gate, g_up, g_down, slot_terms = expert_block(
+        slot_rows, slot_cot, expert_gate[0], expert_up[0], expert_down[0]
+    )
+    low_near, high_near, slot_terms, from_mirror, paired_partial = together(
+        low_near, high_near, slot_terms, from_mirror, paired_partial
+    )
     from_pair = pairs(paired_partial)
-    low_near, high_near, low_kept, high_kept = together(
-        low_near, high_near, low_kept, high_kept
-    )
     low_far = across(add(low_kept[:, :, :width], low_near[:, :, :width]), 4)
     high_far = across(add(high_kept[:, :, :width], high_near[:, :, :width]), 2)
-    low_far, high_far, from_pair, from_mirror = together(
-        low_far, high_far, from_pair, from_mirror
-    )
+    routed = lax.psum_scatter(slot_terms, "ep", scatter_dimension=0, tiled=True)
+    routed_input = slots_back(routed, dispatch, me, experts)
     mine, other = final_sum(
         core, (low_kept, low_near, low_far), (high_kept, high_near, high_far)
     )
+    mine, from_pair = together(mine, from_pair)
     grads = join_halves(core, mine, across(other, 1))
     grad_input = (
         partial0.astype(F32)

time: 297 us -> 288 us (0.970)
  waiting for transfers between devices: 124 us -> 110 us
  Pallas kernels: 72.2 us -> 80.1 us
  other arithmetic: 14.3 us -> 17.9 us
    ppermute x12, waiting for transfers between devices: 27 us -> 1.8 us  [across(): return lax.ppermute(value, 'ep', [(i, i ^ apart) for i in range(8)])]
    ppermute x4, waiting for transfers between devices: 0.01 us -> 21.2 us  [pairs(): return lax.ppermute(value, 'tp', [(0, 1), (1, 0), (2, 3), (3, 2)])]
    ppermute x3 -> x0, waiting for transfers between devices: 12.8 us -> none  [shift(): return lax.ppermute(x, axis, [(i, (i + by) % size) for i in range(size)])]
    reduce_scatter x1, waiting for transfers between devices: 16 us -> 27.1 us  [line_body(): routed = lax.psum_scatter(slot_terms, 'ep', scatter_dimension=0, tiled=True)]
    all_gather x1, waiting for transfers between devices: 7.29 us -> 0.01 us  [line_body(): slots = lax.all_gather(got, 'ep', axis=0, tiled=False)]
    pallas_call x1, Pallas kernels: 19.3 us -> 24.5 us  [expert_block(): pl.pallas_call(kernel, in_specs=[vmem, vmem, hbm, hbm, hbm], out_specs=[h...]
    convert_element_type x3, other arithmetic: 2.17 us -> 7.05 us  [add(): return (a.astype(F32) + b.astype(F32)).astype(BF16)]
    all_to_all x0 -> x1, starting transfers between devices: none -> 4.6 us  [slots_back(): back = lax.all_to_all(own, 'tp', split_axis=0, concat_axis=0, tiled=True)]
  transfers between devices with their start and end apart: 25 -> 23, of which waited for: 10 -> 7; matrix products, arithmetic and copies ran while one was open for 9% -> 10% of each run, Pallas kernels for 23% -> 27%
where the time goes in v2:
time: 288 us; the launch traced here: 286 us
  waiting for transfers between devices  110 us (38%)
  Pallas kernels  80.1 us (28%)
  local copies, waits for them, and re-layouts  39.6 us (14%)
  starting transfers between devices  22.8 us (8%)
  other arithmetic  17.9 us (6%)
  between operations  14.1 us (5%)
    all_to_all x1, waiting for transfers between devices, exchange_slots(): got = lax.all_to_all(sent, 'tp', split_axis=0, concat_axis=0, tiled=True)  34.5 us
    unnamed x68, local copies, waits for them, and re-layouts  31 us
    pallas_call x4, Pallas kernels, weight_terms(): pl.pallas_call(kernel, grid_spec=pltpu.PrefetchScalarGridSpec(num_scalar_...  28.6 us
    reduce_scatter x1, waiting for transfers between devices, line_body(): routed = lax.psum_scatter(slot_terms, 'ep', scatter_dimension=0, tiled=True)  27.1 us
    pallas_call x1, Pallas kernels, expert_block(): pl.pallas_call(kernel, in_specs=[vmem, vmem, hbm, hbm, hbm], out_specs=[h...  24.5 us
    all_gather x1, waiting for transfers between devices, line_body(): down = lax.all_gather(dense_down.T, 'ep', axis=0, tiled=True)  23.9 us
    ppermute x4, waiting for transfers between devices, pairs(): return lax.ppermute(value, 'tp', [(0, 1), (1, 0), (2, 3), (3, 2)])  21.2 us
    pallas_call x3, Pallas kernels, dense_block(): pl.pallas_call(kernel, in_specs=[pl.BlockSpec(memory_space=pltpu.SMEM)] +...  19.7 us
  transfers between devices with their start and end apart: 23, of which 7 were waited for; matrix products, arithmetic and copies ran while one was open for 10% of the time, Pallas kernels for 27%

profile of v2, /device:TPU:0, one launch (start us, length us, event | category | flops | bytes accessed | tf_op | source)
XLA Modules:
  0.0 286.5 jit_solution(12389931915024215440)
XLA Ops:
  7.2 0.7 all-gather.4.cloned.1.call-update
  7.9 1.6 pad_maximum_fusion.refs_0_.refs_6_
  9.6 3.1 %collective-permute-start.3 = (bf16[2,128,3584]{2,1,0:T(8,128)(2,1)S(1)}, bf16[2,128,3584]{2,1,0:T(8,128)(2,1)}, u32[]{:S(2)}, u32[]{:S(2)}) collective-permute-start(bf16[2,128,3584]{2,1,0:T(8,128)(2,1)S(1)} %pad_maximum_fusion.refs_0_.refs_6_), channel_id=1, source_target_pairs={{0,8},{8,0},{16,24},{24,16},{1,9},{9,1},{17,25},{25,17},{2,10},{10... | collective-permute-start | bytes 5505032 | tf_op jit(solution)/shard_map/ppermute | solution.py:372
  12.7 2.5 collective-permute-start.2
  15.6 1.2 reduce-window.6
  18.0 1.1 multiply_reduce_fusion
  21.1 1.4 convolution_convert_fusion
  22.6 1.0 fusion.2
  23.7 3.4 %all-to-all-start = ((bf16[4,2,4,3584]{3,2,1,0:T(4,128)(2,1)}), bf16[4,2,4,3584]{3,2,1,0:T(4,128)(2,1)S(1)}, u32[]{:S(2)}, u32[]{:S(2)}) async-start(bf16[4,2,4,3584]{3,2,1,0:T(4,128)(2,1)} %fusion.2), calls=%async_computation | async-start | bytes 458752 | tf_op jit(solution)/shard_map/all_to_all | solution.py:56
  27.1 23.9 %all-gather.4.cloned.1.call-done.refs_3_.refs_4_ = bf16[3584,608]{1,0:T(8,128)(2,1)} async-done(((bf16[448,608]{1,0:T(8,128)(2,1)}), bf16[3584,608]{1,0:T(8,128)(2,1)}) %all-gather.4.cloned.1.call-update) | async-done | bytes 4358160 | tf_op jit(solution)/shard_map/all_gather | solution.py:369
  51.0 2.3 copy-done.2
  53.3 2.2 copy-done.5
  55.5 2.2 copy-done.8
  57.8 5.0 %dense_block.3 = (bf16[3,304,128]{2,1,0:T(8,128)(2,1)S(1)}, bf16[3,304,128]{2,1,0:T(8,128)(2,1)S(1)}, bf16[128,3584]{1,0:T(8,128)(2,1)S(1)}) custom-call(s32[1]{0:T(128)} %bitcast.6.core_ref, bf16[2,128,3584]{2,1,0:T(8,128)(2,1)S(1)} %pad_maximum_fusion.refs_0_.refs_6_, bf16[608,3584]{1,0:T(8,128)(2,1)S(1)} %copy-done.5, bf16[608,3584]{1,0:T(8,128)(2,1)S(1)} %copy-done.8, ...), custom_call_target="tpu_custom_call" | custom-call | flops 2789212160 | bytes 16293888 | tf_op jit(solution)/shard_map/dense_block/pallas_call | solution.py:155
  62.8 0.7 copy-done.14
  63.5 1.0 copy-done.19
  64.7 34.5 %all-to-all-done = bf16[4,2,4,3584]{3,2,1,0:T(4,128)(2,1)S(1)} async-done(((bf16[4,2,4,3584]{3,2,1,0:T(4,128)(2,1)}), bf16[4,2,4,3584]{3,2,1,0:T(4,128)(2,1)S(1)}, u32[]{:S(2)}, u32[]{:S(2)}) %all-to-all-start) | async-done | bytes 229408 | tf_op jit(solution)/shard_map/all_to_all | solution.py:56
  99.5 0.8 copy.48
  100.5 0.5 collective-permute-start.7
  101.0 2.3 copy-done.3
  103.3 2.2 copy-done.6
  105.6 2.3 copy-done.9
  107.9 9.7 %dense_block.4 = (bf16[3,304,256]{2,1,0:T(8,128)(2,1)S(1)}, bf16[3,304,256]{2,1,0:T(8,128)(2,1)S(1)}, bf16[256,3584]{1,0:T(8,128)(2,1)S(1)}) custom-call(s32[1]{0:T(128)} %bitcast.6.core_ref, bf16[2,128,3584]{2,1,0:T(8,128)(2,1)} %collective-permute-done.3.refs_0_.refs_8_, bf16[2,128,3584]{2,1,0:T(8,128)(2,1)} %collective-permute-done.2.refs_1_.refs_9_, ...), custom_call_target="tpu_custom_call" | custom-call | flops 5578424320 | bytes 19513344 | tf_op jit(solution)/shard_map/dense_block/pallas_call | solution.py:155
  117.6 0.8 copy-done.13
  118.4 1.2 copy-done.16
  119.7 1.8 collective-permute-done.5.refs_3_
  121.5 1.3 copy-done.21
  122.7 1.3 copy-done.22
  124.0 19.3 %collective-permute-done.4.refs_0_.refs_12_ = bf16[2,128,3584]{2,1,0:T(8,128)(2,1)S(1)} collective-permute-done((bf16[2,128,3584]{2,1,0:T(8,128)(2,1)}, bf16[2,128,3584]{2,1,0:T(8,128)(2,1)S(1)}, u32[]{:S(2)}, u32[]{:S(2)}) %collective-permute-start.4) | collective-permute-done | bytes 1835040 | tf_op jit(solution)/shard_map/ppermute | solution.py:372
  143.3 3.0 %copy-done.4 = bf16[3584,608]{1,0:T(8,128)(2,1)S(1)} copy-done((bf16[3584,608]{1,0:T(8,128)(2,1)S(1)}, bf16[3584,608]{1,0:T(8,128)(2,1)}, u32[]{:S(2)}) %copy-start.4) | copy-done | bytes 4358168
  146.2 2.2 copy-done.7
  148.5 2.2 copy-done.10
  150.7 5.0 %dense_block.5 = (bf16[3,304,128]{2,1,0:T(8,128)(2,1)S(1)}, bf16[3,304,128]{2,1,0:T(8,128)(2,1)S(1)}, bf16[128,3584]{1,0:T(8,128)(2,1)S(1)}) custom-call(s32[1]{0:T(128)} %bitcast.6.core_ref, bf16[2,128,3584]{2,1,0:T(8,128)(2,1)S(1)} %collective-permute-done.4.refs_0_.refs_12_, bf16[608,3584]{1,0:T(8,128)(2,1)S(1)} %copy-done.7, ...), custom_call_target="tpu_custom_call" | custom-call | flops 2789212160 | bytes 16293888 | tf_op jit(solution)/shard_map/dense_block/pallas_call | solution.py:155
  155.7 0.7 copy-done.15
  156.7 0.7 pad_add_fusion.3.tile_ref
  157.4 0.7 pad_add_fusion.tile_ref
  158.0 2.2 split.7
  160.2 0.7 copy-done.25
  160.9 7.0 %weight_terms.7 = bf16[3,144,1792]{2,1,0:T(8,128)(2,1)} custom-call(s32[2]{0:T(128)} %pad_add_fusion.3.tile_ref, bf16[3,304,128]{2,1,0:T(8,128)(2,1)} %copy-done.14, bf16[3,304,128]{2,1,0:T(8,128)(2,1)} %copy-done.24, bf16[3,304,256]{2,1,0:T(8,128)(2,1)} %copy-done.13, bf16[3,304,256]{2,1,0:T(8,128)(2,1)} %copy-done.23, bf16[3,304,128]{2,1,0:T(8,128)(2,1)} %copy-done.15, ...), custom_call_target="tpu_custom_call" | custom-call | flops 1585446912 | bytes 10756096 | tf_op jit(solution)/shard_map/weight_terms/pallas_call | solution.py:326
  167.9 1.6 collective-permute-start.12
  169.5 7.2 %weight_terms.4 = bf16[3,160,1792]{2,1,0:T(8,128)(2,1)} custom-call(s32[2]{0:T(128)} %pad_add_fusion.tile_ref, bf16[3,304,128]{2,1,0:T(8,128)(2,1)} %copy-done.14, bf16[3,304,128]{2,1,0:T(8,128)(2,1)} %copy-done.24, bf16[3,304,256]{2,1,0:T(8,128)(2,1)} %copy-done.13, bf16[3,304,256]{2,1,0:T(8,128)(2,1)} %copy-done.23, bf16[3,304,128]{2,1,0:T(8,128)(2,1)} %copy-done.15, ...), custom_call_target="tpu_custom_call" | custom-call | flops 1761607680 | bytes 10928128 | tf_op jit(solution)/shard_map/weight_terms/pallas_call | solution.py:326
  176.7 1.9 collective-permute-done.10
  178.6 1.5 collective-permute-start.11
  180.1 2.4 add_convert_fusion.1
  182.5 2.6 collective-permute-start.13
  185.2 0.6 pad_add_fusion.2.tile_ref
  185.7 0.6 pad_add_fusion.1.tile_ref
  186.3 7.0 %weight_terms.6.refs_3_ = bf16[3,144,1792]{2,1,0:T(8,128)(2,1)} custom-call(s32[2]{0:T(128)} %pad_add_fusion.2.tile_ref, bf16[3,304,128]{2,1,0:T(8,128)(2,1)} %copy-done.14, bf16[3,304,128]{2,1,0:T(8,128)(2,1)} %copy-done.24, bf16[3,304,256]{2,1,0:T(8,128)(2,1)} %copy-done.13, bf16[3,304,256]{2,1,0:T(8,128)(2,1)} %copy-done.23, ...), custom_call_target="tpu_custom_call" | custom-call | flops 1585446912 | bytes 10756096 | tf_op jit(solution)/shard_map/weight_terms/pallas_call | solution.py:326
  193.3 7.4 %weight_terms.5.refs_0_ = bf16[3,160,1792]{2,1,0:T(8,128)(2,1)} custom-call(s32[2]{0:T(128)} %pad_add_fusion.1.tile_ref, bf16[3,304,128]{2,1,0:T(8,128)(2,1)} %copy-done.14, bf16[3,304,128]{2,1,0:T(8,128)(2,1)} %copy-done.24, bf16[3,304,256]{2,1,0:T(8,128)(2,1)} %copy-done.13, bf16[3,304,256]{2,1,0:T(8,128)(2,1)} %copy-done.23, ...), custom_call_target="tpu_custom_call" | custom-call | flops 1761607680 | bytes 10928128 | tf_op jit(solution)/shard_map/weight_terms/pallas_call | solution.py:326
  200.7 1.3 fusion.14
  202.1 24.5 %expert_block.1 = (bf16[608,3584]{1,0:T(8,128)(2,1)}, bf16[608,3584]{1,0:T(8,128)(2,1)}, bf16[608,3584]{1,0:T(8,128)(2,1)}, bf16[128,3584]{1,0:T(8,128)(2,1)}) custom-call(bf16[128,3584]{1,0:T(8,128)(2,1)} %bitcast.50, bf16[128,3584]{1,0:T(8,128)(2,1)} %bitcast.49, bf16[608,3584]{1,0:T(8,128)(2,1)} %bitcast.46, bf16[608,3584]{1,0:T(8,128)(2,1)} %bitcast.47, ...), custom_call_target="tpu_custom_call" | custom-call | flops 1 | bytes 1 | tf_op jit(solution)/shard_map/expert_block/pallas_call | solution.py:228
  226.7 2.4 add_convert_fusion.2
  229.0 1.5 collective-permute-start.14
  230.6 2.3 add_convert_fusion.3
  232.8 0.5 collective-permute-start.15
  233.4 27.1 %reduce-scatter.2.cloned.1.call-done = bf16[16,3584]{1,0:T(8,128)(2,1)} async-done(((bf16[128,3584]{1,0:T(8,128)(2,1)}), bf16[16,3584]{1,0:T(8,128)(2,1)}) %reduce-scatter.2.cloned.1.call-update) | async-done | bytes 114704 | tf_op jit(solution)/shard_map/reduce_scatter | solution.py:430
  260.5 1.6 reshape.109
  262.1 4.6 %all-to-all-start.1 = ((bf16[4,4,3584]{2,1,0:T(4,128)(2,1)}), bf16[4,4,3584]{2,1,0:T(4,128)(2,1)S(1)}, u32[]{:S(2)}, u32[]{:S(2)}) async-start(bf16[4,4,3584]{2,1,0:T(4,128)(2,1)} %reshape.109), calls=%async_computation.2 | async-start | bytes 229376 | tf_op jit(solution)/shard_map/all_to_all | solution.py:79
  266.8 4.4 %final_sum.1 = (bf16[3,304,448]{2,1,0:T(8,128)(2,1)S(1)}, bf16[3,304,448]{2,1,0:T(8,128)(2,1)}) custom-call(s32[1]{0:T(128)} %bitcast.6.core_ref, bf16[3,160,1792]{2,1,0:T(8,128)(2,1)S(1)} %copy-done.11, bf16[3,160,1792]{2,1,0:T(8,128)(2,1)} %collective-permute-done.11.refs_1_, bf16[3,160,896]{2,1,0:T(8,128)(2,1)} %collective-permute-done.14.refs_2_, ...), custom_call_target="tpu_custom_call" | custom-call | flops 2451456 | bytes 6537216 | tf_op jit(solution)/shard_map/final_sum/pallas_call | solution.py:265
  271.2 0.9 copy-done.18
  272.6 0.5 convolution_bitcast_fusion
  273.3 2.8 add_convert_fusion
  276.1 1.0 copy-done.28
  277.1 2.9 %join_halves.1 = (bf16[448,608]{1,0:T(8,128)(2,1)}, bf16[448,608]{1,0:T(8,128)(2,1)}, bf16[448,608]{1,0:T(8,128)(2,1)}) custom-call(s32[1]{0:T(128)} %bitcast.6.core_ref, bf16[3,304,448]{2,1,0:T(8,128)(2,1)} %copy-done.18, bf16[3,304,448]{2,1,0:T(8,128)(2,1)} %copy-done.28), custom_call_target="tpu_custom_call" | custom-call | bytes 3268608 | tf_op jit(solution)/shard_map/join_halves/pallas_call | solution.py:291
  (109 shorter events, 5.7 us)
Async XLA Ops:
  7.2 43.8 %all-gather.4.cloned.1.call-start = ((), (), s32[]{:S(2)}) async-start(), calls=%async_computation.3 | async-start | bytes 5160960 | tf_op jit(solution)/shard_map/all_gather | solution.py:369
  7.9 7.2 %copy-start.31 = (s32[128,2]{0,1:T(2,128)S(1)}, s32[128,2]{0,1:T(2,128)}, u32[]{:S(2)}) copy-start(s32[128,2]{0,1:T(2,128)} %param.12) | copy-start | bytes 3076
  7.9 9.6 %copy-start.32 = (f32[128,2]{0,1:T(2,128)S(1)}, f32[128,2]{0,1:T(2,128)}, u32[]{:S(2)}) copy-start(f32[128,2]{0,1:T(2,128)} %param.13) | copy-start | bytes 3076
  9.6 41.4 %copy-start = (bf16[2,128,3584]{2,1,0:T(8,128)(2,1)}, bf16[2,128,3584]{2,1,0:T(8,128)(2,1)S(1)}, u32[]{:S(2)}) copy-start(bf16[2,128,3584]{2,1,0:T(8,128)(2,1)S(1)} %pad_maximum_fusion.refs_0_.refs_6_) | copy-start | bytes 5505028
  9.6 89.9 %collective-permute-start.3 = (bf16[2,128,3584]{2,1,0:T(8,128)(2,1)S(1)}, bf16[2,128,3584]{2,1,0:T(8,128)(2,1)}, u32[]{:S(2)}, u32[]{:S(2)}) collective-permute-start(bf16[2,128,3584]{2,1,0:T(8,128)(2,1)S(1)} %pad_maximum_fusion.refs_0_.refs_6_), channel_id=1, source_target_pairs={{0,8},{8,0},{16,24},{24,16},{1,9},{9,1},{17,25},{25,17},{2,10},{10... | collective-permute-start | bytes 5505032 | tf_op jit(solution)/shard_map/ppermute | solution.py:372
  12.7 86.8 %collective-permute-start.2 = (bf16[2,128,3584]{2,1,0:T(8,128)(2,1)S(1)}, bf16[2,128,3584]{2,1,0:T(8,128)(2,1)}, u32[]{:S(2)}, u32[]{:S(2)}) collective-permute-start(bf16[2,128,3584]{2,1,0:T(8,128)(2,1)S(1)} %pad_maximum_fusion.refs_0_.refs_6_), channel_id=1, source_target_pairs={{0,24},{8,16},{16,8},{24,0},{1,25},{9,17},{17,9},{25,1},{2,26},{10... | collective-permute-start | bytes 5505032 | tf_op jit(solution)/shard_map/ppermute | solution.py:375
  15.1 84.3 %collective-permute-start.1 = (bf16[2,128,3584]{2,1,0:T(8,128)(2,1)S(1)}, bf16[2,128,3584]{2,1,0:T(8,128)(2,1)}, u32[]{:S(2)}, u32[]{:S(2)}) collective-permute-start(bf16[2,128,3584]{2,1,0:T(8,128)(2,1)S(1)} %pad_maximum_fusion.refs_0_.refs_6_), channel_id=1, source_target_pairs={{0,1},{1,0},{2,3},{3,2},{4,5},{5,4},{6,7},{7,6},{8,9},{9,8},{10,11... | collective-permute-start | bytes 5505032 | tf_op jit(solution)/shard_map/ppermute | solution.py:378
  16.8 4.0 %copy-start.26 = (bf16[128,3584]{1,0:T(8,128)(2,1)S(1)}, bf16[128,3584]{1,0:T(8,128)(2,1)}, u32[]{:S(2)}) copy-start(bf16[128,3584]{1,0:T(8,128)(2,1)} %param.11) | copy-start | bytes 2752516
  20.8 41.9 %copy-start.29 = (bf16[128,16]{1,0:T(8,128)(2,1)}, bf16[128,16]{1,0:T(8,128)(2,1)S(1)}, u32[]{:S(2)}) copy-start(bf16[128,16]{1,0:T(8,128)(2,1)S(1)} %fusion.5) | copy-start | bytes 12292
  23.7 75.5 %all-to-all-start = ((bf16[4,2,4,3584]{3,2,1,0:T(4,128)(2,1)}), bf16[4,2,4,3584]{3,2,1,0:T(4,128)(2,1)S(1)}, u32[]{:S(2)}, u32[]{:S(2)}) async-start(bf16[4,2,4,3584]{3,2,1,0:T(4,128)(2,1)} %fusion.2), calls=%async_computation | async-start | bytes 458752 | tf_op jit(solution)/shard_map/all_to_all | solution.py:56
  27.1 116.2 %all-gather.6.cloned.1.call-start = ((), (), s32[]{:S(2)}) async-start(), calls=%async_computation.5 | async-start | bytes 2064384 | tf_op jit(solution)/shard_map/all_gather | solution.py:398
  51.0 2.3 copy-start.2
  53.3 2.2 copy-start.5
  55.5 2.2 copy-start.8
  62.8 0.7 copy-start.14
  63.5 1.0 copy-start.19
  64.4 35.0 %collective-permute-start = (bf16[3,304,128]{2,1,0:T(8,128)(2,1)S(1)}, bf16[3,304,128]{2,1,0:T(8,128)(2,1)S(1)}, u32[]{:S(2)}, u32[]{:S(2)}) collective-permute-start(bf16[3,304,128]{2,1,0:T(8,128)(2,1)S(1)} %get-tuple-element.57), channel_id=1, source_target_pairs={{0,1},{1,0},{2,3},{3,2},{4,5},{5,4},{6,7},{7,6},{8,9},{9,8},{10,11... | collective-permute-start | bytes 700424 | tf_op jit(solution)/shard_map/ppermute | solution.py:378
  99.4 18.2 %copy-start.24 = (bf16[3,304,128]{2,1,0:T(8,128)(2,1)}, bf16[3,304,128]{2,1,0:T(8,128)(2,1)S(1)}, u32[]{:S(2)}) copy-start(bf16[3,304,128]{2,1,0:T(8,128)(2,1)S(1)} %collective-permute-done.refs_1_) | copy-start | bytes 700420
  100.2 160.3 %reduce-scatter.2.cloned.1.call-start = ((), (), s32[]{:S(2)}) async-start(), calls=%async_computation.4 | async-start | bytes 1032192 | tf_op jit(solution)/shard_map/reduce_scatter | solution.py:430
  100.5 21.0 %collective-permute-start.6 = (bf16[2,128,3584]{2,1,0:T(8,128)(2,1)}, bf16[2,128,3584]{2,1,0:T(8,128)(2,1)S(1)}, u32[]{:S(2)}, u32[]{:S(2)}) collective-permute-start(bf16[2,128,3584]{2,1,0:T(8,128)(2,1)} %collective-permute-done.3.refs_0_.refs_8_), channel_id=1, source_target_pairs={{0,1},{1,0},{2,3},{3,2},{4,5},{5,4},{6,7},{7,6},{8,9},{9,8},{10,11... | collective-permute-start | bytes 5505032 | tf_op jit(solution)/shard_map/ppermute | solution.py:378
  100.5 22.2 %collective-permute-start.7 = (bf16[2,128,3584]{2,1,0:T(8,128)(2,1)}, bf16[2,128,3584]{2,1,0:T(8,128)(2,1)S(1)}, u32[]{:S(2)}, u32[]{:S(2)}) collective-permute-start(bf16[2,128,3584]{2,1,0:T(8,128)(2,1)} %collective-permute-done.2.refs_1_.refs_9_), channel_id=1, source_target_pairs={{0,1},{1,0},{2,3},{3,2},{4,5},{5,4},{6,7},{7,6},{8,9},{9,8},{10,11... | collective-permute-start | bytes 5505032 | tf_op jit(solution)/shard_map/ppermute | solution.py:378
  101.0 42.2 %collective-permute-start.4 = (bf16[2,128,3584]{2,1,0:T(8,128)(2,1)}, bf16[2,128,3584]{2,1,0:T(8,128)(2,1)S(1)}, u32[]{:S(2)}, u32[]{:S(2)}) collective-permute-start(bf16[2,128,3584]{2,1,0:T(8,128)(2,1)} %collective-permute-done.2.refs_1_.refs_9_), channel_id=1, source_target_pairs={{0,8},{8,0},{16,24},{24,16},{1,9},{9,1},{17,25},{25,17},{2,10},{10... | collective-permute-start | bytes 5505032 | tf_op jit(solution)/shard_map/ppermute | solution.py:372
  101.0 2.3 copy-start.3
  103.3 2.2 copy-start.6
  105.6 2.3 copy-start.9
  117.6 0.8 copy-start.13
  118.4 1.2 copy-start.16
  119.6 1.8 collective-permute-start.5
  121.4 34.2 %copy-start.23 = (bf16[3,304,256]{2,1,0:T(8,128)(2,1)}, bf16[3,304,256]{2,1,0:T(8,128)(2,1)S(1)}, u32[]{:S(2)}) copy-start(bf16[3,304,256]{2,1,0:T(8,128)(2,1)S(1)} %collective-permute-done.5.refs_3_) | copy-start | bytes 1400836
  121.5 1.3 copy-start.21
  122.7 1.3 copy-start.22
  143.2 12.5 %copy-start.1 = (bf16[2,128,3584]{2,1,0:T(8,128)(2,1)}, bf16[2,128,3584]{2,1,0:T(8,128)(2,1)S(1)}, u32[]{:S(2)}) copy-start(bf16[2,128,3584]{2,1,0:T(8,128)(2,1)S(1)} %collective-permute-done.4.refs_0_.refs_12_) | copy-start | bytes 5505028
  143.3 16.9 %collective-permute-start.9 = (bf16[2,128,3584]{2,1,0:T(8,128)(2,1)S(1)}, bf16[2,128,3584]{2,1,0:T(8,128)(2,1)}, u32[]{:S(2)}, u32[]{:S(2)}) collective-permute-start(bf16[2,128,3584]{2,1,0:T(8,128)(2,1)S(1)} %collective-permute-done.4.refs_0_.refs_12_), channel_id=1, source_target_pairs={{0,1},{1,0},{2,3},{3,2},{4,5},{5,4},{6,7},{7,6},{8,9},{9,8},{10,11... | collective-permute-start | bytes 5505032 | tf_op jit(solution)/shard_map/ppermute | solution.py:378
  143.3 3.0 %copy-start.4 = (bf16[3584,608]{1,0:T(8,128)(2,1)S(1)}, bf16[3584,608]{1,0:T(8,128)(2,1)}, u32[]{:S(2)}) copy-start(bf16[3584,608]{1,0:T(8,128)(2,1)} %all-gather.4.cloned.1.call-done.refs_3_.refs_4_) | copy-start | bytes 13074436
  146.2 2.2 copy-start.7
  148.5 2.2 copy-start.10
  155.7 0.7 copy-start.15
  156.4 22.2 %collective-permute-start.10 = (bf16[128,3584]{1,0:T(8,128)(2,1)S(1)}, bf16[128,3584]{1,0:T(8,128)(2,1)}, u32[]{:S(2)}, u32[]{:S(2)}) collective-permute-start(bf16[128,3584]{1,0:T(8,128)(2,1)S(1)} %get-tuple-element.79), channel_id=1, source_target_pairs={{0,8},{8,0},{16,24},{24,16},{1,9},{9,1},{17,25},{25,17},{2,10},{10... | collective-permute-start | bytes 2752520 | tf_op jit(solution)/shard_map/ppermute | solution.py:372
  156.7 3.5 %collective-permute-start.8 = (bf16[3,304,128]{2,1,0:T(8,128)(2,1)S(1)}, bf16[3,304,128]{2,1,0:T(8,128)(2,1)S(1)}, u32[]{:S(2)}, u32[]{:S(2)}) collective-permute-start(bf16[3,304,128]{2,1,0:T(8,128)(2,1)S(1)} %get-tuple-element.72), channel_id=1, source_target_pairs={{0,1},{1,0},{2,3},{3,2},{4,5},{5,4},{6,7},{7,6},{8,9},{9,8},{10,11... | collective-permute-start | bytes 700424 | tf_op jit(solution)/shard_map/ppermute | solution.py:378
  160.2 0.7 copy-start.25
  167.9 12.2 %copy-start.17 = (bf16[256,3584]{1,0:T(8,128)(2,1)S(1)}, bf16[256,3584]{1,0:T(8,128)(2,1)}, u32[]{:S(2)}) copy-start(bf16[256,3584]{1,0:T(8,128)(2,1)} %copy-done.16) | copy-start | bytes 5505028
  167.9 58.7 %collective-permute-start.12 = (bf16[3,144,1792]{2,1,0:T(8,128)(2,1)}, bf16[3,144,1792]{2,1,0:T(8,128)(2,1)}, u32[]{:S(2)}, u32[]{:S(2)}) collective-permute-start(bf16[3,144,1792]{2,1,0:T(8,128)(2,1)} %weight_terms.7), channel_id=1, source_target_pairs={{0,4},{1,5},{2,6},{3,7},{4,0},{5,1},{6,2},{7,3},{8,12},{9,13},{10,... | collective-permute-start | bytes 4644872 | tf_op jit(solution)/shard_map/ppermute | solution.py:378
  178.6 48.0 %collective-permute-start.11 = (bf16[3,160,1792]{2,1,0:T(8,128)(2,1)}, bf16[3,160,1792]{2,1,0:T(8,128)(2,1)}, u32[]{:S(2)}, u32[]{:S(2)}) collective-permute-start(bf16[3,160,1792]{2,1,0:T(8,128)(2,1)} %weight_terms.4), channel_id=1, source_target_pairs={{0,2},{1,3},{2,0},{3,1},{4,6},{5,7},{6,4},{7,5},{8,10},{9,11},{10,... | collective-permute-start | bytes 5160968 | tf_op jit(solution)/shard_map/ppermute | solution.py:378
  182.5 44.1 %collective-permute-start.13 = (bf16[128,3584]{1,0:T(8,128)(2,1)}, bf16[128,3584]{1,0:T(8,128)(2,1)}, u32[]{:S(2)}, u32[]{:S(2)}) collective-permute-start(bf16[128,3584]{1,0:T(8,128)(2,1)} %add_convert_fusion.1), channel_id=1, source_target_pairs={{0,24},{8,16},{16,8},{24,0},{1,25},{9,17},{17,9},{25,1},{2,26},{10... | collective-permute-start | bytes 2752520 | tf_op jit(solution)/shard_map/ppermute | solution.py:375
  193.3 7.4 %copy-start.27 = (bf16[16,16,3584]{2,1,0:T(8,128)(2,1)S(1)}, bf16[16,16,3584]{2,1,0:T(8,128)(2,1)}, u32[]{:S(2)}) copy-start(bf16[16,16,3584]{2,1,0:T(8,128)(2,1)} %all-gather.6.cloned.1.call-done) | copy-start | bytes 5505028
  202.0 24.6 %copy-start.11 = (bf16[3,160,1792]{2,1,0:T(8,128)(2,1)S(1)}, bf16[3,160,1792]{2,1,0:T(8,128)(2,1)}, u32[]{:S(2)}) copy-start(bf16[3,160,1792]{2,1,0:T(8,128)(2,1)} %weight_terms.5.refs_0_) | copy-start | bytes 5160964
  226.6 4.0 %copy-start.12 = (bf16[3,144,1792]{2,1,0:T(8,128)(2,1)S(1)}, bf16[3,144,1792]{2,1,0:T(8,128)(2,1)}, u32[]{:S(2)}) copy-start(bf16[3,144,1792]{2,1,0:T(8,128)(2,1)} %weight_terms.6.refs_3_) | copy-start | bytes 4644868
  229.0 37.7 %copy-start.30 = (bf16[128,16]{1,0:T(8,128)(2,1)S(1)}, bf16[128,16]{1,0:T(8,128)(2,1)}, u32[]{:S(2)}) copy-start(bf16[128,16]{1,0:T(8,128)(2,1)} %copy-done.29) | copy-start | bytes 12292
  229.0 37.7 %collective-permute-start.14 = (bf16[3,160,896]{2,1,0:T(8,128)(2,1)}, bf16[3,160,896]{2,1,0:T(8,128)(2,1)}, u32[]{:S(2)}, u32[]{:S(2)}) collective-permute-start(bf16[3,160,896]{2,1,0:T(8,128)(2,1)} %add_convert_fusion.2), channel_id=1, source_target_pairs={{0,4},{1,5},{2,6},{3,7},{4,0},{5,1},{6,2},{7,3},{8,12},{9,13},{10,... | collective-permute-start | bytes 2580488 | tf_op jit(solution)/shard_map/ppermute | solution.py:378
  230.6 41.6 %collective-permute-start.16 = (bf16[128,3584]{1,0:T(8,128)(2,1)}, bf16[128,3584]{1,0:T(8,128)(2,1)}, u32[]{:S(2)}, u32[]{:S(2)}) collective-permute-start(bf16[128,3584]{1,0:T(8,128)(2,1)} %split.7), channel_id=1, source_target_pairs={{0,8},{8,0},{16,24},{24,16},{1,9},{9,1},{17,25},{25,17},{2,10},{10... | collective-permute-start | bytes 2752520 | tf_op jit(solution)/shard_map/ppermute | solution.py:372
  232.8 33.9 %collective-permute-start.15 = (bf16[3,144,896]{2,1,0:T(8,128)(2,1)}, bf16[3,144,896]{2,1,0:T(8,128)(2,1)}, u32[]{:S(2)}, u32[]{:S(2)}) collective-permute-start(bf16[3,144,896]{2,1,0:T(8,128)(2,1)} %add_convert_fusion.3), channel_id=1, source_target_pairs={{0,2},{1,3},{2,0},{3,1},{4,6},{5,7},{6,4},{7,5},{8,10},{9,11},{10,... | collective-permute-start | bytes 2322440 | tf_op jit(solution)/shard_map/ppermute | solution.py:378
  262.1 10.5 %all-to-all-start.1 = ((bf16[4,4,3584]{2,1,0:T(4,128)(2,1)}), bf16[4,4,3584]{2,1,0:T(4,128)(2,1)S(1)}, u32[]{:S(2)}, u32[]{:S(2)}) async-start(bf16[4,4,3584]{2,1,0:T(4,128)(2,1)} %reshape.109), calls=%async_computation.2 | async-start | bytes 229376 | tf_op jit(solution)/shard_map/all_to_all | solution.py:79
  271.2 0.9 copy-start.18
  272.1 1.2 copy-start.20
  272.1 4.0 %collective-permute-start.17 = (bf16[3,304,448]{2,1,0:T(8,128)(2,1)}, bf16[3,304,448]{2,1,0:T(8,128)(2,1)S(1)}, u32[]{:S(2)}, u32[]{:S(2)}) collective-permute-start(bf16[3,304,448]{2,1,0:T(8,128)(2,1)} %get-tuple-element.96), channel_id=1, source_target_pairs={{0,1},{1,0},{2,3},{3,2},{4,5},{5,4},{6,7},{7,6},{8,9},{9,8},{10,11... | collective-permute-start | bytes 2451464 | tf_op jit(solution)/shard_map/ppermute | solution.py:378
  276.1 1.0 copy-start.28
Sparse Core Ops, SparseCore 0:
  9.9 41.0 all-gather.3
  100.4 27.0 all-gather.5
  226.8 33.6 reduce-scatter.1

commit v3 on v2

--- a/solution.py
+++ b/solution.py
@@ -105,7 +105,7 @@
     return [(start, min(256, units - start)) for start in range(0, units, 256)]
 
 
-def layer_kernel(rows, cots, gate, up, down, down_turned, turned, partial, col, ready=None):
+def layer_kernel(rows, cots, gate, up, down, down_turned, turned, partials, col, ready=None):
     units, width = gate.shape
     for t, (start, size) in enumerate(unit_tiles(units)):
         if ready is not None:
@@ -126,10 +126,15 @@
             turned[i, start : start + size] = value
     grads = [turned[1].T, turned[2].T]
     for j in range(0, width, col):
-        partial[:, j : j + col] = (
+        made = (
             jnp.dot(grads[0], gate[:, j : j + col], preferred_element_type=F32)
             + jnp.dot(grads[1], up[:, j : j + col], preferred_element_type=F32)
         ).astype(BF16)
+        begin = 0
+        for partial in partials:
+            end = begin + partial.shape[0]
+            partial[:, j : j + col] = made[begin:end]
+            begin = end
 
 
 def dense_block(core, blocks, gate, up, down):
@@ -139,14 +144,15 @@
 
     def kernel(core_ref, *refs):
         ins, refs = refs[: len(blocks)], refs[len(blocks) :]
-        gate, up, down, own, other, partial, turned = refs
+        gate, up, down, own, other = refs[:5]
+        partials, turned = refs[5:-1], refs[-1]
         rows, cots = [
             ins[0][k]
             if len(ins) == 1
             else jnp.concatenate([ref[k] for ref in ins], axis=0)
             for k in range(2)
         ]
-        layer_kernel(rows, cots, gate, up, down, True, turned, partial, 512)
+        layer_kernel(rows, cots, gate, up, down, True, turned, partials, 512)
         mine = core_ref[0]
         own[...] = turned[:, pl.ds(pl.multiple_of(mine * half, 16), half), :]
         other[...] = turned[:, pl.ds(pl.multiple_of((1 - mine) * half, 16), half), :]
@@ -155,11 +161,11 @@
     return pl.pallas_call(
         kernel,
         in_specs=[pl.BlockSpec(memory_space=pltpu.SMEM)] + [vmem] * (len(blocks) + 3),
-        out_specs=[vmem, vmem, vmem],
+        out_specs=[vmem] * (2 + len(blocks)),
         out_shape=[
             jax.ShapeDtypeStruct((3, half, tok), BF16),
             jax.ShapeDtypeStruct((3, half, tok), BF16),
-            jax.ShapeDtypeStruct((tok, width), BF16),
+            *[jax.ShapeDtypeStruct(b.shape[1:], BF16) for b in blocks],
         ],
         scratch_shapes=[pltpu.VMEM((3, units, tok), BF16)],
         compiler_params=pltpu.CompilerParams(vmem_limit_bytes=VMEM_LIMIT),
@@ -199,7 +205,7 @@
                 copy.wait()
 
         layer_kernel(
-            rows[...], cots[...], *[loaded.at[w] for w in range(3)], False, turned, partial, 512, ready
+            rows[...], cots[...], *[loaded.at[w] for w in range(3)], False, turned, (partial,), 512, ready
         )
         outs = (g_down, g_gate, g_up)
         pending = [None, None]
@@ -339,7 +345,50 @@
             transcendentals=0,
         ),
         name="weight_terms",
-    )(jnp.stack(tiles), *acts, *blocks)
+    )(tiles, *acts, *blocks)
+
+
+def routed_rows(hidden_in, cotangent, routes, gate_values, experts):
+    tok, width = hidden_in.shape
+    count = experts * 2 * CAP
+
+    def kernel(rows, cots, routes, gates, out):
+        line = lax.broadcasted_iota(jnp.int32, (count, tok), 0)
+        expert, slot = line // (2 * CAP), lax.rem(line, CAP)
+        first, second = routes[0:1] == expert, routes[1:2] == expert
+        named = jnp.where(first | second, 1.0, 0.0)
+        earlier = lax.broadcasted_iota(jnp.int32, (tok, tok), 0) < lax.broadcasted_iota(
+            jnp.int32, (tok, tok), 1
+        )
+        before = jnp.dot(
+            named.astype(BF16),
+            jnp.where(earlier, 1.0, 0.0).astype(BF16),
+            preferred_element_type=F32,
+        )
+        taken = jnp.where(before == slot.astype(F32), named, 0.0)
+        weight = jnp.where(first, gates[0:1], 0.0) + jnp.where(second, gates[1:2], 0.0)
+        weight = jnp.sum(taken * weight, axis=1, keepdims=True)
+        taken = taken.astype(BF16)
+        kept = lax.broadcasted_iota(jnp.int32, (count, 1), 0)
+        is_cot = lax.rem(kept, 2 * CAP) >= CAP
+        for j in range(0, width, 512):
+            columns = slice(j, j + 512)
+            row_part = jnp.dot(taken, rows[:, columns], preferred_element_type=F32)
+            cot_part = jnp.dot(taken, cots[:, columns], preferred_element_type=F32) * weight
+            out[:, columns] = jnp.where(is_cot, cot_part, row_part).astype(BF16)
+
+    vmem = pl.BlockSpec(memory_space=pltpu.VMEM)
+    return pl.pallas_call(
+        kernel,
+        in_specs=[vmem] * 4,
+        out_specs=vmem,
+        out_shape=jax.ShapeDtypeStruct((count, width), BF16),
+        compiler_params=pltpu.CompilerParams(vmem_limit_bytes=VMEM_LIMIT),
+        cost_estimate=pl.CostEstimate(
+            flops=4 * count * tok * width, bytes_accessed=4 * tok * width, transcendentals=0
+        ),
+        name="routed_rows",
+    )(hidden_in, cotangent, routes.T, gate_values.T)
 
 
 def together(*values):
@@ -364,8 +413,6 @@
     core, chip = lax.rem(ep, 2), lax.div(ep, 2)
     half = dense_gate.shape[0] // 2
     columns = dense_down.shape[1]
-    own = jnp.stack([hidden_in, cotangent])
-
     down = lax.all_gather(dense_down.T, "ep", axis=0, tiled=True)
 
     def pairs(value):
@@ -381,53 +428,55 @@
         return (a.astype(F32) + b.astype(F32)).astype(BF16)
 
     def dense(blocks):
-        mine, other, partial = dense_block(core, blocks, dense_gate, dense_up, down)
+        mine, other, *partials = dense_block(core, blocks, dense_gate, dense_up, down)
         tokens = [*blocks, *(across(b, 1) for b in blocks)]
-        return ([mine, across(other, 1)], tokens), partial
-
+        return ([mine, across(other, 1)], tokens), partials
+
+    sent = routed_rows(hidden_in, cotangent, routes, gate_values, experts)
+    got = lax.all_to_all(sent, "tp", split_axis=0, concat_axis=0, tiled=True)
+
+    own, got = together(jnp.stack([hidden_in, cotangent]), got)
     mirrored, paired = mirror(own), pairs(own)
-    dispatch, weight = slot_tables(routes, gate_values, me, experts)
-    sent = slots_to_send(hidden_in, cotangent, dispatch, weight, experts)
-    got = exchange_slots(sent, me, experts)
-    both0, partial0 = dense([own])
-
-    got, partial0, both0 = together(got, partial0, both0)
-
-    mirrored, paired, got = together(mirrored, paired, got)
+    slots = lax.all_gather(got, "ep", axis=0, tiled=False)
+    both0, (partial0,) = dense([own])
+    dispatch, _ = slot_tables(routes, gate_values, me, experts)
+    slots = slots.reshape(-1, 2, CAP, hidden_in.shape[1])
+    slot_rows, slot_cot = [slots[:, k].reshape(-1, hidden_in.shape[1]) for k in range(2)]
+    g_gate, g_up, g_down, slot_terms = expert_block(
+        slot_rows, slot_cot, expert_gate[0], expert_up[0], expert_down[0]
+    )
+    x_chip, y_chip, xy_chip = [jnp.bitwise_xor(chip, k) for k in (1, 2, 3)]
+    chip_tiles = [
+        jnp.stack(t)
+        for t in ((xy_chip, x_chip), (xy_chip, y_chip), (y_chip, chip), (x_chip, chip))
+    ]
+
+    mirrored, paired, slot_terms, both0, dispatch, chip_tiles = together(
+        mirrored, paired, slot_terms, both0, dispatch, chip_tiles
+    )
+    routed = lax.psum_scatter(slot_terms, "ep", scatter_dimension=0, tiled=True)
     last = pairs(mirrored)
-    slots = lax.all_gather(got, "ep", axis=0, tiled=False)
-    both12, partial12 = dense([paired, mirrored])
-
-    last, both12, slots = together(last, both12, slots)
-    both3, partial3 = dense([last])
-    paired_partial, mirrored_partial = jnp.split(partial12, 2, axis=0)
+    both12, (paired_partial, mirrored_partial) = dense([paired, mirrored])
+
+    last, both12, routed = together(last, both12, routed)
+    both3, (partial3,) = dense([last])
     from_last = pairs(partial3)
 
     acts, tokens = (a + b + c for a, b, c in zip(both0, both12, both3))
     cut, width = -(-half // 32) * 16, 2 * columns
-    x_chip, y_chip, xy_chip = [jnp.bitwise_xor(chip, k) for k in (1, 2, 3)]
-    low_sent = weight_terms((xy_chip, x_chip), acts, tokens, width, 0, cut)
-    high_sent = weight_terms((xy_chip, y_chip), acts, tokens, width, cut, half)
-    low_sent, chip, from_last = together(low_sent, chip, from_last)
-    low_kept = weight_terms((y_chip, chip), acts, tokens, width, 0, cut)
-    high_kept = weight_terms((x_chip, chip), acts, tokens, width, cut, half)
+    low_sent = weight_terms(chip_tiles[0], acts, tokens, width, 0, cut)
+    high_sent = weight_terms(chip_tiles[1], acts, tokens, width, cut, half)
+    low_sent, chip_tiles, from_last = together(low_sent, chip_tiles, from_last)
+    low_kept = weight_terms(chip_tiles[2], acts, tokens, width, 0, cut)
+    high_kept = weight_terms(chip_tiles[3], acts, tokens, width, cut, half)
     low_near, high_near = across(low_sent, 2), across(high_sent, 4)
     from_mirror = mirror(add(mirrored_partial, from_last))
-
-    slots, low_kept, high_kept = together(slots, low_kept, high_kept)
-    slot_rows, slot_cot = slots[:, 0].reshape(-1, hidden_in.shape[1]), slots[:, 1].reshape(
-        -1, hidden_in.shape[1]
-    )
-    g_gate, g_up, g_down, slot_terms = expert_block(
-        slot_rows, slot_cot, expert_gate[0], expert_up[0], expert_down[0]
-    )
-    low_near, high_near, slot_terms, from_mirror, paired_partial = together(
-        low_near, high_near, slot_terms, from_mirror, paired_partial
+    low_near, high_near, low_kept, high_kept, from_mirror, paired_partial, routed = together(
+        low_near, high_near, low_kept, high_kept, from_mirror, paired_partial, routed
     )
     from_pair = pairs(paired_partial)
     low_far = across(add(low_kept[:, :, :width], low_near[:, :, :width]), 4)
     high_far = across(add(high_kept[:, :, :width], high_near[:, :, :width]), 2)
-    routed = lax.psum_scatter(slot_terms, "ep", scatter_dimension=0, tiled=True)
     routed_input = slots_back(routed, dispatch, me, experts)
     mine, other = final_sum(
         core, (low_kept, low_near, low_far), (high_kept, high_near, high_far)

time: 288 us -> 305 us (1.059)
  waiting for transfers between devices: 110 us -> 119 us
  starting transfers between devices: 22.8 us -> 31.3 us
  local copies, waits for them, and re-layouts: 39.6 us -> 43.9 us
    all_to_all x1, waiting for transfers between devices: 34.5 us -> 6.83 us  [line_body(): got = lax.all_to_all(sent, 'tp', split_axis=0, concat_axis=0, tiled=True)]
    all_gather x1, waiting for transfers between devices: 0.01 us -> 18.2 us  [line_body(): slots = lax.all_gather(got, 'ep', axis=0, tiled=False)]
    reduce_scatter x1, waiting for transfers between devices: 27.1 us -> 13.4 us  [line_body(): routed = lax.psum_scatter(slot_terms, 'ep', scatter_dimension=0, tiled=True)]
    all_to_all x1, waiting for transfers between devices: 0.43 us -> 14 us  [slots_back(): back = lax.all_to_all(own, 'tp', split_axis=0, concat_axis=0, tiled=True)]
    ppermute x12, waiting for transfers between devices: 1.8 us -> 15 us  [across(): return lax.ppermute(value, 'ep', [(i, i ^ apart) for i in range(8)])]
    ppermute x4, waiting for transfers between devices: 21.2 us -> 8.43 us  [pairs(): return lax.ppermute(value, 'tp', [(0, 1), (1, 0), (2, 3), (3, 2)])]
    all_gather x1, waiting for transfers between devices: 23.9 us -> 36.2 us  [line_body(): down = lax.all_gather(dense_down.T, 'ep', axis=0, tiled=True)]
    ppermute x4, starting transfers between devices: 3.37 us -> 10.3 us  [pairs(): return lax.ppermute(value, 'tp', [(0, 1), (1, 0), (2, 3), (3, 2)])]
  transfers between devices with their start and end apart: 23 -> 23, of which waited for: 7 -> 11; matrix products, arithmetic and copies ran while one was open for 10% -> 8% of each run, Pallas kernels for 27% -> 25%
where the time goes in v3:
time: 305 us; the launch traced here: 304 us
  waiting for transfers between devices  119 us (39%)
  Pallas kernels  80.7 us (26%)
  local copies, waits for them, and re-layouts  43.9 us (14%)
  starting transfers between devices  31.3 us (10%)
  other arithmetic  14.9 us (5%)
  between operations  14.1 us (5%)
    all_gather x1, waiting for transfers between devices, line_body(): down = lax.all_gather(dense_down.T, 'ep', axis=0, tiled=True)  36.2 us
    unnamed x75, local copies, waits for them, and re-layouts  31.8 us
    pallas_call x4, Pallas kernels, weight_terms(): pl.pallas_call(kernel, grid_spec=pltpu.PrefetchScalarGridSpec(num_scalar_...  28.4 us
    pallas_call x1, Pallas kernels, expert_block(): pl.pallas_call(kernel, in_specs=[vmem, vmem, hbm, hbm, hbm], out_specs=[h...  24.4 us
    pallas_call x3, Pallas kernels, dense_block(): pl.pallas_call(kernel, in_specs=[pl.BlockSpec(memory_space=pltpu.SMEM)] +...  21 us
    all_gather x1, waiting for transfers between devices, line_body(): slots = lax.all_gather(got, 'ep', axis=0, tiled=False)  18.2 us
    ppermute x12, waiting for transfers between devices, across(): return lax.ppermute(value, 'ep', [(i, i ^ apart) for i in range(8)])  15 us
    all_to_all x1, waiting for transfers between devices, slots_back(): back = lax.all_to_all(own, 'tp', split_axis=0, concat_axis=0, tiled=True)  14 us
  transfers between devices with their start and end apart: 23, of which 11 were waited for; matrix products, arithmetic and copies ran while one was open for 8% of the time, Pallas kernels for 25%

profile of v3, /device:TPU:0, one launch (start us, length us, event | category | flops | bytes accessed | tf_op | source)
XLA Modules:
  0.0 304.0 jit_solution(17680264675583682587)
XLA Ops:
  7.2 1.2 copy-done.18
  8.3 1.2 copy-done.20
  9.5 0.7 copy-done.26
  10.9 1.2 routed_rows.1
  12.1 6.3 %all-to-all-start = ((bf16[4,8,3584]{2,1,0:T(8,128)(2,1)}), bf16[4,8,3584]{2,1,0:T(8,128)(2,1)S(1)}, u32[]{:S(2)}, u32[]{:S(2)}) async-start(bf16[4,8,3584]{2,1,0:T(8,128)(2,1)} %bitcast.5), calls=%async_computation | async-start | bytes 458752 | tf_op jit(solution)/shard_map/all_to_all | solution.py:436
  18.4 1.4 pad_maximum_fusion.refs_0_.refs_6_
  19.8 6.8 %all-to-all-done = bf16[4,8,3584]{2,1,0:T(8,128)(2,1)S(1)} async-done(((bf16[4,8,3584]{2,1,0:T(8,128)(2,1)}), bf16[4,8,3584]{2,1,0:T(8,128)(2,1)S(1)}, u32[]{:S(2)}, u32[]{:S(2)}) %all-to-all-start) | async-done | bytes 229408 | tf_op jit(solution)/shard_map/all_to_all | solution.py:436
  26.6 0.7 copy-done.35
  27.4 0.7 all-gather.4.cloned.1.call-update
  28.6 1.2 reduce-window.6
  30.6 1.2 collective-permute-start
  35.2 18.2 %all-gather.6.cloned.1.call-done = bf16[256,3584]{1,0:T(8,128)(2,1)} async-done(((bf16[32,3584]{1,0:T(8,128)(2,1)}), bf16[256,3584]{1,0:T(8,128)(2,1)}) %all-gather.6.cloned.1.call-update) | async-done | bytes 1835024 | tf_op jit(solution)/shard_map/all_gather | solution.py:440
  53.4 4.0 %reshape.100 = bf16[32,2,4,3584]{3,2,1,0:T(4,128)(2,1)} reshape(bf16[256,3584]{1,0:T(8,128)(2,1)} %all-gather.6.cloned.1.call-done) | data formatting | bytes 3670016 | tf_op jit(solution)/shard_map/reshape | solution.py:443
  57.5 36.2 %all-gather.4.cloned.1.call-done.refs_3_.refs_4_ = bf16[3584,608]{1,0:T(8,128)(2,1)} async-done(((bf16[448,608]{1,0:T(8,128)(2,1)}), bf16[3584,608]{1,0:T(8,128)(2,1)}) %all-gather.4.cloned.1.call-update) | async-done | bytes 4358160 | tf_op jit(solution)/shard_map/all_gather | solution.py:416
  93.7 2.3 copy-done.2
  96.0 2.2 copy-done.5
  98.2 2.2 copy-done.8
  100.5 5.1 %dense_block.3 = (bf16[3,304,128]{2,1,0:T(8,128)(2,1)S(1)}, bf16[3,304,128]{2,1,0:T(8,128)(2,1)S(1)}, bf16[128,3584]{1,0:T(8,128)(2,1)S(1)}) custom-call(s32[1]{0:T(128)} %bitcast.core_ref, bf16[2,128,3584]{2,1,0:T(8,128)(2,1)S(1)} %pad_maximum_fusion.refs_0_.refs_6_, bf16[608,3584]{1,0:T(8,128)(2,1)S(1)} %copy-done.5, bf16[608,3584]{1,0:T(8,128)(2,1)S(1)} %copy-done.8, ...), custom_call_target="tpu_custom_call" | custom-call | flops 2789212160 | bytes 16293888 | tf_op jit(solution)/shard_map/dense_block/pallas_call | solution.py:161
  105.9 1.6 fusion.8
  107.5 2.4 reshape_squeeze.7.cots
  109.9 1.1 reshape_squeeze.6.rows
  111.0 24.4 %expert_block.1 = (bf16[608,3584]{1,0:T(8,128)(2,1)}, bf16[608,3584]{1,0:T(8,128)(2,1)}, bf16[608,3584]{1,0:T(8,128)(2,1)}, bf16[128,3584]{1,0:T(8,128)(2,1)}) custom-call(bf16[128,3584]{1,0:T(8,128)(2,1)} %reshape_squeeze.6.rows, bf16[128,3584]{1,0:T(8,128)(2,1)} %reshape_squeeze.7.cots, bf16[608,3584]{1,0:T(8,128)(2,1)} %bitcast.43, ...), custom_call_target="tpu_custom_call" | custom-call | flops 1 | bytes 1 | tf_op jit(solution)/shard_map/expert_block/pallas_call | solution.py:234
  136.0 1.5 collective-permute-start.4
  137.6 2.3 copy-done.3
  139.9 2.2 copy-done.6
  142.1 2.3 copy-done.9
  144.4 10.8 %dense_block.4 = (bf16[3,304,256]{2,1,0:T(8,128)(2,1)S(1)}, bf16[3,304,256]{2,1,0:T(8,128)(2,1)S(1)}, bf16[128,3584]{1,0:T(8,128)(2,1)}, bf16[128,3584]{1,0:T(8,128)(2,1)S(1)}) custom-call(s32[1]{0:T(128)} %bitcast.core_ref, bf16[2,128,3584]{2,1,0:T(8,128)(2,1)} %collective-permute-done.1.refs_0_.refs_8_, ...), custom_call_target="tpu_custom_call" | custom-call | flops 5578424320 | bytes 19513344 | tf_op jit(solution)/shard_map/dense_block/pallas_call | solution.py:161
  155.3 0.8 copy-done.13
  156.0 1.0 copy-done.24
  157.0 1.8 collective-permute-done.5.refs_3_
  158.8 13.4 %reduce-scatter.2.cloned.1.call-done = bf16[16,3584]{1,0:T(8,128)(2,1)} async-done(((bf16[128,3584]{1,0:T(8,128)(2,1)}), bf16[16,3584]{1,0:T(8,128)(2,1)}) %reduce-scatter.2.cloned.1.call-update) | async-done | bytes 114704 | tf_op jit(solution)/shard_map/reduce_scatter | solution.py:457
  172.3 6.1 %collective-permute-done.4.refs_0_.refs_12_ = bf16[2,128,3584]{2,1,0:T(8,128)(2,1)S(1)} collective-permute-done((bf16[2,128,3584]{2,1,0:T(8,128)(2,1)}, bf16[2,128,3584]{2,1,0:T(8,128)(2,1)S(1)}, u32[]{:S(2)}, u32[]{:S(2)}) %collective-permute-start.4) | collective-permute-done | bytes 1835040 | tf_op jit(solution)/shard_map/ppermute | solution.py:419
  178.4 3.0 copy-done.4
  181.4 2.2 copy-done.7
  183.6 2.2 copy-done.10
  185.8 5.1 %dense_block.5 = (bf16[3,304,128]{2,1,0:T(8,128)(2,1)S(1)}, bf16[3,304,128]{2,1,0:T(8,128)(2,1)S(1)}, bf16[128,3584]{1,0:T(8,128)(2,1)S(1)}) custom-call(s32[1]{0:T(128)} %bitcast.core_ref, bf16[2,128,3584]{2,1,0:T(8,128)(2,1)S(1)} %collective-permute-done.4.refs_0_.refs_12_, bf16[608,3584]{1,0:T(8,128)(2,1)S(1)} %copy-done.7, ...), custom_call_target="tpu_custom_call" | custom-call | flops 2789212160 | bytes 16293888 | tf_op jit(solution)/shard_map/dense_block/pallas_call | solution.py:161
  191.0 0.7 copy-done.17
  191.6 1.5 collective-permute-start.10
  193.1 1.5 collective-permute-done.8.refs_5_
  194.6 1.3 copy-done.29
  195.9 7.0 %weight_terms.5 = bf16[3,144,1792]{2,1,0:T(8,128)(2,1)} custom-call(s32[2]{0:T(128)} %get-tuple-element.86.tile_ref, bf16[3,304,128]{2,1,0:T(8,128)(2,1)} %copy-done.16, bf16[3,304,128]{2,1,0:T(8,128)(2,1)} %copy-done.32, bf16[3,304,256]{2,1,0:T(8,128)(2,1)} %copy-done.13, bf16[3,304,256]{2,1,0:T(8,128)(2,1)} %copy-done.30, bf16[3,304,128]{2,1,0:T(8,128)(2,1)} %copy-done.17, ...), custom_call_target="tpu_custom_call" | custom-call | flops 1585446912 | bytes 10756096 | tf_op jit(solution)/shard_map/weight_terms/pallas_call | solution.py:332
  202.9 1.4 collective-permute-start.12
  204.3 7.2 %weight_terms.4 = bf16[3,160,1792]{2,1,0:T(8,128)(2,1)} custom-call(s32[2]{0:T(128)} %get-tuple-element.67.tile_ref, bf16[3,304,128]{2,1,0:T(8,128)(2,1)} %copy-done.16, bf16[3,304,128]{2,1,0:T(8,128)(2,1)} %copy-done.32, bf16[3,304,256]{2,1,0:T(8,128)(2,1)} %copy-done.13, bf16[3,304,256]{2,1,0:T(8,128)(2,1)} %copy-done.30, bf16[3,304,128]{2,1,0:T(8,128)(2,1)} %copy-done.17, ...), custom_call_target="tpu_custom_call" | custom-call | flops 1761607680 | bytes 10928128 | tf_op jit(solution)/shard_map/weight_terms/pallas_call | solution.py:332
  211.5 2.3 collective-permute-done.10
  213.9 1.5 collective-permute-start.11
  215.3 2.3 add_convert_fusion.1
  217.6 3.3 %collective-permute-start.13 = (bf16[128,3584]{1,0:T(8,128)(2,1)}, bf16[128,3584]{1,0:T(8,128)(2,1)}, u32[]{:S(2)}, u32[]{:S(2)}) collective-permute-start(bf16[128,3584]{1,0:T(8,128)(2,1)} %add_convert_fusion.1), channel_id=1, source_target_pairs={{0,24},{8,16},{16,8},{24,0},{1,25},{9,17},{17,9},{25,1},{2,26},{10... | collective-permute-start | bytes 2752520 | tf_op jit(solution)/shard_map/ppermute | solution.py:422
  221.0 7.0 %weight_terms.7.refs_3_ = bf16[3,144,1792]{2,1,0:T(8,128)(2,1)} custom-call(s32[2]{0:T(128)} %get-tuple-element.92.tile_ref, bf16[3,304,128]{2,1,0:T(8,128)(2,1)} %copy-done.16, bf16[3,304,128]{2,1,0:T(8,128)(2,1)} %copy-done.32, bf16[3,304,256]{2,1,0:T(8,128)(2,1)} %copy-done.13, bf16[3,304,256]{2,1,0:T(8,128)(2,1)} %copy-done.30, ...), custom_call_target="tpu_custom_call" | custom-call | flops 1585446912 | bytes 10756096 | tf_op jit(solution)/shard_map/weight_terms/pallas_call | solution.py:332
  228.0 7.2 %weight_terms.6.refs_0_ = bf16[3,160,1792]{2,1,0:T(8,128)(2,1)} custom-call(s32[2]{0:T(128)} %get-tuple-element.91.tile_ref, bf16[3,304,128]{2,1,0:T(8,128)(2,1)} %copy-done.16, bf16[3,304,128]{2,1,0:T(8,128)(2,1)} %copy-done.32, bf16[3,304,256]{2,1,0:T(8,128)(2,1)} %copy-done.13, bf16[3,304,256]{2,1,0:T(8,128)(2,1)} %copy-done.30, ...), custom_call_target="tpu_custom_call" | custom-call | flops 1761607680 | bytes 10928128 | tf_op jit(solution)/shard_map/weight_terms/pallas_call | solution.py:332
  235.2 5.6 %collective-permute-done.13 = bf16[128,3584]{1,0:T(8,128)(2,1)} collective-permute-done((bf16[128,3584]{1,0:T(8,128)(2,1)}, bf16[128,3584]{1,0:T(8,128)(2,1)}, u32[]{:S(2)}, u32[]{:S(2)}) %collective-permute-start.13) | collective-permute-done | bytes 917536 | tf_op jit(solution)/shard_map/ppermute | solution.py:422
  240.8 11.7 %collective-permute-done.11.refs_1_ = bf16[3,160,1792]{2,1,0:T(8,128)(2,1)S(1)} collective-permute-done((bf16[3,160,1792]{2,1,0:T(8,128)(2,1)}, bf16[3,160,1792]{2,1,0:T(8,128)(2,1)S(1)}, u32[]{:S(2)}, u32[]{:S(2)}) %collective-permute-start.11) | collective-permute-done | bytes 1720352 | tf_op jit(solution)/shard_map/ppermute | solution.py:425
  252.5 2.9 add_convert_fusion.2
  255.4 1.3 collective-permute-start.14
  256.7 6.9 %collective-permute-start.16 = (bf16[128,3584]{1,0:T(8,128)(2,1)}, bf16[128,3584]{1,0:T(8,128)(2,1)}, u32[]{:S(2)}, u32[]{:S(2)}) collective-permute-start(bf16[128,3584]{1,0:T(8,128)(2,1)} %get-tuple-element.102), channel_id=1, source_target_pairs={{0,8},{8,0},{16,24},{24,16},{1,9},{9,1},{17,25},{25,17},{2,10},{10... | collective-permute-start | bytes 2752520 | tf_op jit(solution)/shard_map/ppermute | solution.py:419
  263.6 2.2 add_convert_fusion.3
  265.9 1.3 collective-permute-start.15
  267.1 0.7 reshape.103
  267.8 3.7 %all-to-all-start.1 = ((bf16[4,4,3584]{2,1,0:T(4,128)(2,1)}), bf16[4,4,3584]{2,1,0:T(4,128)(2,1)S(1)}, u32[]{:S(2)}, u32[]{:S(2)}) async-start(bf16[4,4,3584]{2,1,0:T(4,128)(2,1)} %reshape.103), calls=%async_computation.2 | async-start | bytes 229376 | tf_op jit(solution)/shard_map/all_to_all | solution.py:79
  271.6 14.0 %all-to-all-done.1 = bf16[4,4,3584]{2,1,0:T(4,128)(2,1)S(1)} async-done(((bf16[4,4,3584]{2,1,0:T(4,128)(2,1)}), bf16[4,4,3584]{2,1,0:T(4,128)(2,1)S(1)}, u32[]{:S(2)}, u32[]{:S(2)}) %all-to-all-start.1) | async-done | bytes 114720 | tf_op jit(solution)/shard_map/all_to_all | solution.py:79
  286.1 1.5 copy-done.15
  287.5 2.9 final_sum.1
  290.5 3.1 %add_convert_fusion = bf16[128,3584]{1,0:T(8,128)(2,1)} fusion(f32[128,3584]{1,0:T(8,128)S(1)} %convolution_bitcast_fusion, bf16[128,3584]{1,0:T(8,128)(2,1)} %collective-permute-done.13, bf16[128,3584]{1,0:T(8,128)(2,1)} %collective-permute-done.16, bf16[128,3584]{1,0:T(8,128)(2,1)S(1)} %copy-done.23), kind=kLoop, calls=%fused_computation.2 | loop fusion | flops 3211264 | bytes 5505024 | tf_op jit(solution)/shard_map/convert_element_type | solution.py:491
  293.6 1.0 copy-done.34
  294.6 2.9 join_halves.1
  (107 shorter events, 7.1 us)
Async XLA Ops:
  7.2 1.2 copy-start.18
  8.3 1.2 copy-start.20
  9.5 0.7 copy-start.26
  10.2 0.7 copy-start.28
  10.9 7.5 %copy-start.19 = (bf16[128,3584]{1,0:T(8,128)(2,1)S(1)}, bf16[128,3584]{1,0:T(8,128)(2,1)}, u32[]{:S(2)}) copy-start(bf16[128,3584]{1,0:T(8,128)(2,1)} %rows.1) | copy-start | bytes 2752516
  12.1 14.5 %all-to-all-start = ((bf16[4,8,3584]{2,1,0:T(8,128)(2,1)}), bf16[4,8,3584]{2,1,0:T(8,128)(2,1)S(1)}, u32[]{:S(2)}, u32[]{:S(2)}) async-start(bf16[4,8,3584]{2,1,0:T(8,128)(2,1)} %bitcast.5), calls=%async_computation | async-start | bytes 458752 | tf_op jit(solution)/shard_map/all_to_all | solution.py:436
  18.4 35.0 %all-gather.6.cloned.1.call-start = ((), (), s32[]{:S(2)}) async-start(), calls=%async_computation.5 | async-start | bytes 2064384 | tf_op jit(solution)/shard_map/all_gather | solution.py:440
  18.4 9.7 %copy-start.27 = (s32[128,2]{0,1:T(2,128)S(1)}, s32[128,2]{0,1:T(2,128)}, u32[]{:S(2)}) copy-start(s32[128,2]{0,1:T(2,128)} %param.12) | copy-start | bytes 3076
  19.8 73.9 %copy-start = (bf16[2,128,3584]{2,1,0:T(8,128)(2,1)}, bf16[2,128,3584]{2,1,0:T(8,128)(2,1)S(1)}, u32[]{:S(2)}) copy-start(bf16[2,128,3584]{2,1,0:T(8,128)(2,1)S(1)} %pad_maximum_fusion.refs_0_.refs_6_) | copy-start | bytes 5505028
  26.6 0.7 copy-start.35
  27.3 66.4 %all-gather.4.cloned.1.call-start = ((), (), s32[]{:S(2)}) async-start(), calls=%async_computation.3 | async-start | bytes 5160960 | tf_op jit(solution)/shard_map/all_gather | solution.py:416
  28.1 144.2 %reduce-scatter.2.cloned.1.call-start = ((), (), s32[]{:S(2)}) async-start(), calls=%async_computation.4 | async-start | bytes 1032192 | tf_op jit(solution)/shard_map/reduce_scatter | solution.py:457
  30.2 105.2 %collective-permute-start.3 = (bf16[2,128,3584]{2,1,0:T(8,128)(2,1)S(1)}, bf16[2,128,3584]{2,1,0:T(8,128)(2,1)}, u32[]{:S(2)}, u32[]{:S(2)}) collective-permute-start(bf16[2,128,3584]{2,1,0:T(8,128)(2,1)S(1)} %pad_maximum_fusion.refs_0_.refs_6_), channel_id=1, source_target_pairs={{0,1},{1,0},{2,3},{3,2},{4,5},{5,4},{6,7},{7,6},{8,9},{9,8},{10,11... | collective-permute-start | bytes 5505032 | tf_op jit(solution)/shard_map/ppermute | solution.py:425
  30.2 105.2 %collective-permute-start.1 = (bf16[2,128,3584]{2,1,0:T(8,128)(2,1)S(1)}, bf16[2,128,3584]{2,1,0:T(8,128)(2,1)}, u32[]{:S(2)}, u32[]{:S(2)}) collective-permute-start(bf16[2,128,3584]{2,1,0:T(8,128)(2,1)S(1)} %pad_maximum_fusion.refs_0_.refs_6_), channel_id=1, source_target_pairs={{0,8},{8,0},{16,24},{24,16},{1,9},{9,1},{17,25},{25,17},{2,10},{10... | collective-permute-start | bytes 5505032 | tf_op jit(solution)/shard_map/ppermute | solution.py:419
  30.6 104.8 %collective-permute-start = (bf16[2,128,3584]{2,1,0:T(8,128)(2,1)S(1)}, bf16[2,128,3584]{2,1,0:T(8,128)(2,1)}, u32[]{:S(2)}, u32[]{:S(2)}) collective-permute-start(bf16[2,128,3584]{2,1,0:T(8,128)(2,1)S(1)} %pad_maximum_fusion.refs_0_.refs_6_), channel_id=1, source_target_pairs={{0,24},{8,16},{16,8},{24,0},{1,25},{9,17},{17,9},{25,1},{2,26},{10... | collective-permute-start | bytes 5505032 | tf_op jit(solution)/shard_map/ppermute | solution.py:422
  93.7 2.3 copy-start.2
  96.0 2.2 copy-start.5
  98.2 2.2 copy-start.8
  100.5 5.4 %copy-start.31 = (bf16[32,2,4,3584]{3,2,1,0:T(4,128)(2,1)S(1)}, bf16[32,2,4,3584]{3,2,1,0:T(4,128)(2,1)}, u32[]{:S(2)}) copy-start(bf16[32,2,4,3584]{3,2,1,0:T(4,128)(2,1)} %reshape.100) | copy-start | bytes 5505028
  105.5 1.9 copy-start.16
  105.6 1.9 copy-start.22
  105.6 29.9 %collective-permute-start.2 = (bf16[3,304,128]{2,1,0:T(8,128)(2,1)S(1)}, bf16[3,304,128]{2,1,0:T(8,128)(2,1)S(1)}, u32[]{:S(2)}, u32[]{:S(2)}) collective-permute-start(bf16[3,304,128]{2,1,0:T(8,128)(2,1)S(1)} %get-tuple-element.66), channel_id=1, source_target_pairs={{0,1},{1,0},{2,3},{3,2},{4,5},{5,4},{6,7},{7,6},{8,9},{9,8},{10,11... | collective-permute-start | bytes 700424 | tf_op jit(solution)/shard_map/ppermute | solution.py:425
  135.4 19.8 %copy-start.32 = (bf16[3,304,128]{2,1,0:T(8,128)(2,1)}, bf16[3,304,128]{2,1,0:T(8,128)(2,1)S(1)}, u32[]{:S(2)}) copy-start(bf16[3,304,128]{2,1,0:T(8,128)(2,1)S(1)} %collective-permute-done.2.refs_1_) | copy-start | bytes 700420
  135.5 36.8 %collective-permute-start.6 = (bf16[2,128,3584]{2,1,0:T(8,128)(2,1)}, bf16[2,128,3584]{2,1,0:T(8,128)(2,1)}, u32[]{:S(2)}, u32[]{:S(2)}) collective-permute-start(bf16[2,128,3584]{2,1,0:T(8,128)(2,1)} %collective-permute-done.1.refs_0_.refs_8_), channel_id=1, source_target_pairs={{0,1},{1,0},{2,3},{3,2},{4,5},{5,4},{6,7},{7,6},{8,9},{9,8},{10,11... | collective-permute-start | bytes 5505032 | tf_op jit(solution)/shard_map/ppermute | solution.py:425
  135.8 36.5 %collective-permute-start.7 = (bf16[2,128,3584]{2,1,0:T(8,128)(2,1)}, bf16[2,128,3584]{2,1,0:T(8,128)(2,1)}, u32[]{:S(2)}, u32[]{:S(2)}) collective-permute-start(bf16[2,128,3584]{2,1,0:T(8,128)(2,1)} %collective-permute-done.refs_1_.refs_9_), channel_id=1, source_target_pairs={{0,1},{1,0},{2,3},{3,2},{4,5},{5,4},{6,7},{7,6},{8,9},{9,8},{10,11... | collective-permute-start | bytes 5505032 | tf_op jit(solution)/shard_map/ppermute | solution.py:425
  136.0 42.4 %collective-permute-start.4 = (bf16[2,128,3584]{2,1,0:T(8,128)(2,1)}, bf16[2,128,3584]{2,1,0:T(8,128)(2,1)S(1)}, u32[]{:S(2)}, u32[]{:S(2)}) collective-permute-start(bf16[2,128,3584]{2,1,0:T(8,128)(2,1)} %collective-permute-done.refs_1_.refs_9_), channel_id=1, source_target_pairs={{0,8},{8,0},{16,24},{24,16},{1,9},{9,1},{17,25},{25,17},{2,10},{10... | collective-permute-start | bytes 5505032 | tf_op jit(solution)/shard_map/ppermute | solution.py:419
  137.6 2.3 copy-start.3
  139.9 2.2 copy-start.6
  142.1 2.3 copy-start.9
  155.3 0.8 copy-start.13
  156.0 1.0 copy-start.24
  157.0 1.8 collective-permute-start.5
  158.8 32.1 %copy-start.30 = (bf16[3,304,256]{2,1,0:T(8,128)(2,1)}, bf16[3,304,256]{2,1,0:T(8,128)(2,1)S(1)}, u32[]{:S(2)}) copy-start(bf16[3,304,256]{2,1,0:T(8,128)(2,1)S(1)} %collective-permute-done.5.refs_3_) | copy-start | bytes 1400836
  178.4 12.5 %copy-start.1 = (bf16[2,128,3584]{2,1,0:T(8,128)(2,1)}, bf16[2,128,3584]{2,1,0:T(8,128)(2,1)S(1)}, u32[]{:S(2)}) copy-start(bf16[2,128,3584]{2,1,0:T(8,128)(2,1)S(1)} %collective-permute-done.4.refs_0_.refs_12_) | copy-start | bytes 5505028
  178.4 16.2 %collective-permute-start.9 = (bf16[2,128,3584]{2,1,0:T(8,128)(2,1)S(1)}, bf16[2,128,3584]{2,1,0:T(8,128)(2,1)S(1)}, u32[]{:S(2)}, u32[]{:S(2)}) collective-permute-start(bf16[2,128,3584]{2,1,0:T(8,128)(2,1)S(1)} %collective-permute-done.4.refs_0_.refs_12_), channel_id=1, source_target_pairs={{0,1},{1,0},{2,3},{3,2},{4,5},{5,4},{6,7},{7,6},{8,9},{9,8},{10,11... | collective-permute-start | bytes 5505032 | tf_op jit(solution)/shard_map/ppermute | solution.py:425
  178.4 3.0 copy-start.4
  181.4 2.2 copy-start.7
  183.6 2.2 copy-start.10
  190.9 0.7 copy-start.17
  191.6 22.2 %collective-permute-start.10 = (bf16[128,3584]{1,0:T(8,128)(2,1)S(1)}, bf16[128,3584]{1,0:T(8,128)(2,1)}, u32[]{:S(2)}, u32[]{:S(2)}) collective-permute-start(bf16[128,3584]{1,0:T(8,128)(2,1)S(1)} %get-tuple-element.89), channel_id=1, source_target_pairs={{0,8},{8,0},{16,24},{24,16},{1,9},{9,1},{17,25},{25,17},{2,10},{10... | collective-permute-start | bytes 2752520 | tf_op jit(solution)/shard_map/ppermute | solution.py:419
  193.1 1.5 collective-permute-start.8
  194.6 1.3 copy-start.33
  194.6 1.3 copy-start.29
  202.9 12.4 %copy-start.25 = (bf16[128,3584]{1,0:T(8,128)(2,1)S(1)}, bf16[128,3584]{1,0:T(8,128)(2,1)}, u32[]{:S(2)}) copy-start(bf16[128,3584]{1,0:T(8,128)(2,1)} %copy-done.24) | copy-start | bytes 2752516
  202.9 37.9 %collective-permute-start.12 = (bf16[3,144,1792]{2,1,0:T(8,128)(2,1)}, bf16[3,144,1792]{2,1,0:T(8,128)(2,1)}, u32[]{:S(2)}, u32[]{:S(2)}) collective-permute-start(bf16[3,144,1792]{2,1,0:T(8,128)(2,1)} %weight_terms.5), channel_id=1, source_target_pairs={{0,4},{1,5},{2,6},{3,7},{4,0},{5,1},{6,2},{7,3},{8,12},{9,13},{10,... | collective-permute-start | bytes 4644872 | tf_op jit(solution)/shard_map/ppermute | solution.py:425
  213.9 38.7 %collective-permute-start.11 = (bf16[3,160,1792]{2,1,0:T(8,128)(2,1)}, bf16[3,160,1792]{2,1,0:T(8,128)(2,1)S(1)}, u32[]{:S(2)}, u32[]{:S(2)}) collective-permute-start(bf16[3,160,1792]{2,1,0:T(8,128)(2,1)} %weight_terms.4), channel_id=1, source_target_pairs={{0,2},{1,3},{2,0},{3,1},{4,6},{5,7},{6,4},{7,5},{8,10},{9,11},{10,... | collective-permute-start | bytes 5160968 | tf_op jit(solution)/shard_map/ppermute | solution.py:425
  217.6 23.2 %collective-permute-start.13 = (bf16[128,3584]{1,0:T(8,128)(2,1)}, bf16[128,3584]{1,0:T(8,128)(2,1)}, u32[]{:S(2)}, u32[]{:S(2)}) collective-permute-start(bf16[128,3584]{1,0:T(8,128)(2,1)} %add_convert_fusion.1), channel_id=1, source_target_pairs={{0,24},{8,16},{16,8},{24,0},{1,25},{9,17},{17,9},{25,1},{2,26},{10... | collective-permute-start | bytes 2752520 | tf_op jit(solution)/shard_map/ppermute | solution.py:422
  235.2 28.4 %copy-start.12 = (bf16[3,144,1792]{2,1,0:T(8,128)(2,1)S(1)}, bf16[3,144,1792]{2,1,0:T(8,128)(2,1)}, u32[]{:S(2)}) copy-start(bf16[3,144,1792]{2,1,0:T(8,128)(2,1)} %weight_terms.7.refs_3_) | copy-start | bytes 4644868
  252.5 11.1 %copy-start.14 = (bf16[3,160,1792]{2,1,0:T(8,128)(2,1)}, bf16[3,160,1792]{2,1,0:T(8,128)(2,1)S(1)}, u32[]{:S(2)}) copy-start(bf16[3,160,1792]{2,1,0:T(8,128)(2,1)S(1)} %collective-permute-done.11.refs_1_) | copy-start | bytes 5160964
  252.5 14.6 %copy-start.36 = (bf16[16,3584]{1,0:T(8,128)(2,1)S(1)}, bf16[16,3584]{1,0:T(8,128)(2,1)}, u32[]{:S(2)}) copy-start(bf16[16,3584]{1,0:T(8,128)(2,1)} %reduce-scatter.2.cloned.1.call-done) | copy-start | bytes 344068
  255.4 30.6 %collective-permute-start.14 = (bf16[3,160,896]{2,1,0:T(8,128)(2,1)}, bf16[3,160,896]{2,1,0:T(8,128)(2,1)}, u32[]{:S(2)}, u32[]{:S(2)}) collective-permute-start(bf16[3,160,896]{2,1,0:T(8,128)(2,1)} %add_convert_fusion.2), channel_id=1, source_target_pairs={{0,4},{1,5},{2,6},{3,7},{4,0},{5,1},{6,2},{7,3},{8,12},{9,13},{10,... | collective-permute-start | bytes 2580488 | tf_op jit(solution)/shard_map/ppermute | solution.py:425
  256.7 33.8 %collective-permute-start.16 = (bf16[128,3584]{1,0:T(8,128)(2,1)}, bf16[128,3584]{1,0:T(8,128)(2,1)}, u32[]{:S(2)}, u32[]{:S(2)}) collective-permute-start(bf16[128,3584]{1,0:T(8,128)(2,1)} %get-tuple-element.102), channel_id=1, source_target_pairs={{0,8},{8,0},{16,24},{24,16},{1,9},{9,1},{17,25},{25,17},{2,10},{10... | collective-permute-start | bytes 2752520 | tf_op jit(solution)/shard_map/ppermute | solution.py:419
  265.9 20.2 %copy-start.11 = (bf16[3,160,1792]{2,1,0:T(8,128)(2,1)S(1)}, bf16[3,160,1792]{2,1,0:T(8,128)(2,1)}, u32[]{:S(2)}) copy-start(bf16[3,160,1792]{2,1,0:T(8,128)(2,1)} %weight_terms.6.refs_0_) | copy-start | bytes 5160964
  265.9 20.2 %collective-permute-start.15 = (bf16[3,144,896]{2,1,0:T(8,128)(2,1)}, bf16[3,144,896]{2,1,0:T(8,128)(2,1)}, u32[]{:S(2)}, u32[]{:S(2)}) collective-permute-start(bf16[3,144,896]{2,1,0:T(8,128)(2,1)} %add_convert_fusion.3), channel_id=1, source_target_pairs={{0,2},{1,3},{2,0},{3,1},{4,6},{5,7},{6,4},{7,5},{8,10},{9,11},{10,... | collective-permute-start | bytes 2322440 | tf_op jit(solution)/shard_map/ppermute | solution.py:425
  267.8 17.7 %all-to-all-start.1 = ((bf16[4,4,3584]{2,1,0:T(4,128)(2,1)}), bf16[4,4,3584]{2,1,0:T(4,128)(2,1)S(1)}, u32[]{:S(2)}, u32[]{:S(2)}) async-start(bf16[4,4,3584]{2,1,0:T(4,128)(2,1)} %reshape.103), calls=%async_computation.2 | async-start | bytes 229376 | tf_op jit(solution)/shard_map/all_to_all | solution.py:79
  285.5 5.0 %copy-start.23 = (bf16[128,3584]{1,0:T(8,128)(2,1)S(1)}, bf16[128,3584]{1,0:T(8,128)(2,1)}, u32[]{:S(2)}) copy-start(bf16[128,3584]{1,0:T(8,128)(2,1)} %copy-done.22) | copy-start | bytes 2752516
  286.1 1.5 copy-start.15
  290.4 3.2 %copy-start.21 = (bf16[3,304,448]{2,1,0:T(8,128)(2,1)}, bf16[3,304,448]{2,1,0:T(8,128)(2,1)S(1)}, u32[]{:S(2)}) copy-start(bf16[3,304,448]{2,1,0:T(8,128)(2,1)S(1)} %get-tuple-element.107.mine) | copy-start | bytes 2451460
  290.4 3.2 %collective-permute-start.17 = (bf16[3,304,448]{2,1,0:T(8,128)(2,1)S(1)}, bf16[3,304,448]{2,1,0:T(8,128)(2,1)S(1)}, u32[]{:S(2)}, u32[]{:S(2)}) collective-permute-start(bf16[3,304,448]{2,1,0:T(8,128)(2,1)S(1)} %get-tuple-element.108), channel_id=1, source_target_pairs={{0,1},{1,0},{2,3},{3,2},{4,5},{5,4},{6,7},{7,6},{8,9},{9,8},{10,11... | collective-permute-start | bytes 2451464 | tf_op jit(solution)/shard_map/ppermute | solution.py:425
  293.6 1.0 copy-start.34
Sparse Core Ops, SparseCore 0:
  27.4 25.9 all-gather.5
  55.3 38.3 all-gather.3
  137.7 34.5 reduce-scatter.1
